TPU v7x, 32 devices: a whole 2x2x4 slice. The times are simulated.
32 devices in a mesh: stream: 2 (over x), batch: 16 (over z, y, core).
Axes of the slice: x: 2, y: 2, z: 4, core: 2. Of those that a mesh axis runs over, the one named last changes fastest.
Arguments:
- features: bfloat16 [2, 32, 512, 768], P('stream', 'batch'), may hold values from -6 to 6
- cotangent: bfloat16 [2, 32, 512, 768], P('stream', 'batch'), may hold values from -6 to 6
- segment_ids: int32 [32, 512], P('batch'), may hold values from 0 to 3, never falling along the last dimension, each value on 1 to 256 neighbouring positions
- box_cells: int32 [2, 32, 2, 512], P('stream', 'batch'), may hold values from 0 to 15
- ln_gain: float32 [2, 2, 768], P('stream'), may hold values from 0.5 to 1.5
- ln_shift: float32 [2, 2, 768], P('stream'), may hold values from -1.8 to 1.8
- w_qkv: bfloat16 [2, 768, 2304], P('stream'), may hold values from -0.21875 to 0.21875
- attn_bias: float32 [2, 3, 768], P('stream'), may hold values from -1.8 to 1.8
- distance_table: float32 [2, 64, 12], P('stream'), may hold values from -4 to 4
- w_out: bfloat16 [2, 768, 768], P('stream'), may hold values from -1.25 to 1.25
- w_up: bfloat16 [2, 768, 3072], P('stream'), may hold values from -0.21875 to 0.21875
- up_bias: float32 [2, 3072], P('stream'), may hold values from -1.8 to 1.8
- w_down: bfloat16 [2, 3072, 768], P('stream'), may hold values from -0.109375 to 0.109375
- down_bias: float32 [2, 768], P('stream'), may hold values from -1.8 to 1.8
Outputs:
- output: bfloat16 [2, 32, 512, 768], P('stream', 'batch')
- input_grad: bfloat16 [2, 32, 512, 768], P('stream', 'batch')
- grad_ln_gain: float32 [2, 2, 768], P('stream')
- grad_ln_shift: float32 [2, 2, 768], P('stream')
- grad_w_qkv: float32 [2, 768, 2304], P('stream')
- grad_attn_bias: float32 [2, 3, 768], P('stream')
- grad_distance_table: float32 [2, 64, 12], P('stream')
- grad_w_out: float32 [2, 768, 768], P('stream')
- grad_w_up: float32 [2, 768, 3072], P('stream')
- grad_up_bias: float32 [2, 3072], P('stream')
- grad_w_down: float32 [2, 3072, 768], P('stream')
- grad_down_bias: float32 [2, 768], P('stream')
Inputs may be any that keep to these rules, and one draw needn't show every extreme that they name: `segment_ids`: along each row the document numbers never fall; every document has 1 to 256 tokens and one has 256.
All inputs are finite; a program needn't handle non-finite values.
Results may differ from a plain program's by a relative error of at most 0.015.
Values may be sent and summed in bfloat16 or wider, within the bound.
A program may use at most 320 MiB of HBM per device.

v0:
```python
import jax
import jax.numpy as jnp
from jax import lax
from jax.sharding import PartitionSpec as P

GRID = 8


EPSILON = 1e-05
MASKED = -1000000000.0


def from_partner(block, axis, stride):
    count = lax.axis_size(axis)
    route = []
    for low in range(count):
        high = low | 1 << stride
        if high != low and high < count:
            route += [(low, high), (high, low)]
    return lax.ppermute(block, axis, route)


def layer_norm(values, norm_gain, norm_shift):
    center = values - jnp.mean(values, axis=-1, keepdims=True)
    spread = jnp.mean(center * center, axis=-1, keepdims=True)
    return center * lax.rsqrt(spread + EPSILON) * norm_gain + norm_shift


def norm_back(values, norm_gain, norm_shift, upstream):
    unused, pull_back = jax.vjp(layer_norm, values, norm_gain, norm_shift)
    return pull_back(upstream)


def gelu_exact(values):
    return jax.nn.gelu(values, approximate=False)


def gelu_back(values, upstream):
    unused, pull_back = jax.vjp(gelu_exact, values)
    return pull_back(upstream)[0]


def split_heads(matrix, heads_count):
    return matrix.reshape(matrix.shape[0], heads_count, matrix.shape[1] // heads_count)


def bucket_onehot(box_row):
    step_x = jnp.minimum(jnp.abs(box_row[0][:, None] - box_row[0][None, :]), GRID - 1)
    step_y = jnp.minimum(jnp.abs(box_row[1][:, None] - box_row[1][None, :]), GRID - 1)
    bucket_codes = (step_x * GRID + step_y).reshape(1, -1)
    return (bucket_codes == lax.broadcasted_iota(jnp.int32, (GRID * GRID, 1), 0)).astype(
        jnp.bfloat16
    )


def split_table(bias_table):
    table_high = bias_table.astype(jnp.bfloat16)
    table_low = (bias_table - table_high.astype(jnp.float32)).astype(jnp.bfloat16)
    return jnp.concatenate([table_high, table_low], axis=1).T


def bias_block(onehot, table_parts, allowed):
    length = allowed.shape[0]
    heads_count = table_parts.shape[0] // 2
    looked_both = jnp.dot(table_parts, onehot, preferred_element_type=jnp.float32)
    looked = (looked_both[:heads_count] + looked_both[heads_count:]).reshape(
        heads_count, length, length
    )
    masked_bias = jnp.where(allowed[None], looked, MASKED)
    return jnp.concatenate([masked_bias, jnp.zeros_like(masked_bias)], axis=2)


def score_block(queries, keys_all, extra_bias, heads_count):
    head_scale = (queries.shape[1] // heads_count) ** (-0.5)
    raw_scores = jnp.einsum(
        "qhd,khd->hqk",
        split_heads(queries, heads_count),
        split_heads(keys_all, heads_count),
        preferred_element_type=jnp.float32,
    )
    return raw_scores * head_scale + extra_bias


def on_device(
    features,
    cotangent,
    segment_ids,
    box_cells,
    ln_gain,
    ln_shift,
    w_qkv,
    attn_bias,
    distance_table,
    w_out,
    w_up,
    up_bias,
    w_down,
    down_bias,
):
    row_count, length, model_width = (features.shape[1], features.shape[2], features.shape[3])
    tokens = row_count * length
    heads_count = distance_table.shape[2]
    head_scale = (model_width // heads_count) ** (-0.5)
    is_vision = lax.axis_index("stream") != 0
    norm_gains, norm_shifts = (ln_gain[0], ln_shift[0])
    bias_table = distance_table[0]
    table_parts = split_table(bias_table)
    bias_rows = attn_bias[0]
    qkv_weight, out_weight, up_weight, down_weight = (w_qkv[0], w_out[0], w_up[0], w_down[0])
    box_rows = box_cells[0]
    plain_in = features[0].reshape(tokens, model_width).astype(jnp.float32)
    normed = layer_norm(plain_in, norm_gains[0], norm_shifts[0]).astype(jnp.bfloat16)
    combined = jnp.dot(normed, qkv_weight, preferred_element_type=jnp.float32)
    queries = (combined[:, :model_width] + bias_rows[0]).astype(jnp.bfloat16)
    key_part = combined[:, model_width : 2 * model_width].astype(jnp.bfloat16)
    value_part = (combined[:, 2 * model_width :] + bias_rows[1]).astype(jnp.bfloat16)
    own_pair = jnp.stack([key_part, value_part])
    partner = from_partner(own_pair, "stream", 0)

    def by_row(matrix):
        return matrix.reshape(row_count, length, matrix.shape[-1])

    def allowed_of(segment_row):
        return jnp.logical_or(segment_row[:, None] == segment_row[None, :], is_vision)

    def forward_row(row_items):
        row_query, row_key, row_value, far_key, far_value, segment_row, box_row = row_items
        extra_bias = bias_block(bucket_onehot(box_row), table_parts, allowed_of(segment_row))
        keys_all = jnp.concatenate([row_key, far_key], axis=0)
        values_all = jnp.concatenate([row_value, far_value], axis=0)
        scores = score_block(row_query, keys_all, extra_bias, heads_count)
        row_max = jnp.max(scores, axis=2, keepdims=True)
        exponent = jnp.exp(scores - row_max)
        row_sum = jnp.sum(exponent, axis=2, keepdims=True)
        probabilities = (exponent / row_sum).astype(jnp.bfloat16)
        mixed_heads = jnp.einsum(
            "hqk,khd->qhd",
            probabilities,
            split_heads(values_all, heads_count),
            preferred_element_type=jnp.float32,
        )
        return (
            mixed_heads.reshape(length, model_width).astype(jnp.bfloat16),
            (row_max + jnp.log(row_sum))[:, :, 0],
        )

    attended, log_sums = lax.map(
        forward_row,
        (
            by_row(queries),
            by_row(key_part),
            by_row(value_part),
            by_row(partner[0]),
            by_row(partner[1]),
            segment_ids,
            box_rows,
        ),
    )
    attended = attended.reshape(tokens, model_width)
    middle = (
        plain_in + jnp.dot(attended, out_weight, preferred_element_type=jnp.float32) + bias_rows[2]
    )
    normed_two = layer_norm(middle, norm_gains[1], norm_shifts[1]).astype(jnp.bfloat16)
    pre_act = jnp.dot(normed_two, up_weight, preferred_element_type=jnp.float32) + up_bias[0]
    activated = gelu_exact(pre_act).astype(jnp.bfloat16)
    result = (
        middle + jnp.dot(activated, down_weight, preferred_element_type=jnp.float32) + down_bias[0]
    )
    output = result.astype(jnp.bfloat16).reshape(1, row_count, length, model_width)
    cot_bf = cotangent[0].reshape(tokens, model_width)
    cot_f32 = cot_bf.astype(jnp.float32)
    grad_down = jnp.einsum("tf,td->fd", activated, cot_bf, preferred_element_type=jnp.float32)
    grad_down_bias = jnp.sum(cot_f32, axis=0)
    grad_act = jnp.einsum("td,fd->tf", cot_bf, down_weight, preferred_element_type=jnp.float32)
    grad_pre = gelu_back(pre_act, grad_act).astype(jnp.bfloat16)
    grad_up = jnp.einsum("td,tf->df", normed_two, grad_pre, preferred_element_type=jnp.float32)
    grad_up_bias = jnp.sum(grad_pre.astype(jnp.float32), axis=0)
    grad_normed_two = jnp.einsum(
        "tf,df->td", grad_pre, up_weight, preferred_element_type=jnp.float32
    )
    grad_mid_part, gain_two, shift_two = norm_back(
        middle, norm_gains[1], norm_shifts[1], grad_normed_two
    )
    grad_middle = cot_f32 + grad_mid_part
    ffn_sums = (grad_up, grad_down, grad_up_bias, grad_down_bias)
    grad_branch = grad_middle.astype(jnp.bfloat16)
    grad_out = jnp.einsum("td,te->de", attended, grad_branch, preferred_element_type=jnp.float32)
    grad_out_bias = jnp.sum(grad_branch.astype(jnp.float32), axis=0)
    grad_attended = jnp.einsum(
        "te,de->td", grad_branch, out_weight, preferred_element_type=jnp.float32
    ).astype(jnp.bfloat16)

    def backward_row(row_items):
        (
            row_query,
            row_key,
            row_value,
            far_key,
            far_value,
            row_grad,
            row_log_sum,
            segment_row,
            box_row,
        ) = row_items
        onehot = bucket_onehot(box_row)
        extra_bias = bias_block(onehot, table_parts, allowed_of(segment_row))
        keys_all = jnp.concatenate([row_key, far_key], axis=0)
        values_all = jnp.concatenate([row_value, far_value], axis=0)
        scores = score_block(row_query, keys_all, extra_bias, heads_count)
        probabilities = jnp.exp(scores - row_log_sum[:, :, None])
        grad_heads = split_heads(row_grad, heads_count)
        grad_probs = jnp.einsum(
            "qhd,khd->hqk",
            grad_heads,
            split_heads(values_all, heads_count),
            preferred_element_type=jnp.float32,
        )
        inner_sum = jnp.sum(probabilities * grad_probs, axis=2, keepdims=True)
        grad_scores = (probabilities * (grad_probs - inner_sum)).astype(jnp.bfloat16)
        grad_query = (
            jnp.einsum(
                "hqk,khd->qhd",
                grad_scores,
                split_heads(keys_all, heads_count),
                preferred_element_type=jnp.float32,
            ).reshape(length, model_width)
            * head_scale
        )
        grad_keys = (
            jnp.einsum(
                "hqk,qhd->khd",
                grad_scores,
                split_heads(row_query, heads_count),
                preferred_element_type=jnp.float32,
            ).reshape(2 * length, model_width)
            * head_scale
        )
        grad_values = jnp.einsum(
            "hqk,qhd->khd",
            probabilities.astype(jnp.bfloat16),
            grad_heads,
            preferred_element_type=jnp.float32,
        ).reshape(2 * length, model_width)
        near_grad = grad_scores[:, :, :length].reshape(heads_count, length * length)
        grad_table = jnp.einsum("hp,np->hn", near_grad, onehot, preferred_element_type=jnp.float32)
        return (grad_query, grad_keys, grad_values, grad_table)

    grad_query, grad_keys, grad_values, grad_table = lax.map(
        backward_row,
        (
            by_row(queries),
            by_row(key_part),
            by_row(value_part),
            by_row(partner[0]),
            by_row(partner[1]),
            by_row(grad_attended),
            log_sums,
            segment_ids,
            box_rows,
        ),
    )
    far_grads = jnp.stack(
        [
            grad_keys[:, length:].reshape(tokens, model_width),
            grad_values[:, length:].reshape(tokens, model_width),
        ]
    )
    returned = from_partner(far_grads.astype(jnp.bfloat16), "stream", 0).astype(far_grads.dtype)
    grad_q_bf = grad_query.reshape(tokens, model_width).astype(jnp.bfloat16)
    grad_k_bf = (grad_keys[:, :length].reshape(tokens, model_width) + returned[0]).astype(
        jnp.bfloat16
    )
    grad_v_bf = (grad_values[:, :length].reshape(tokens, model_width) + returned[1]).astype(
        jnp.bfloat16
    )
    grad_mixed = jnp.concatenate([grad_q_bf, grad_k_bf, grad_v_bf], axis=1)
    grad_qkv = jnp.einsum("td,te->de", normed, grad_mixed, preferred_element_type=jnp.float32)
    grad_bias_rows = jnp.stack(
        [
            jnp.sum(grad_q_bf.astype(jnp.float32), axis=0),
            jnp.sum(grad_v_bf.astype(jnp.float32), axis=0),
            grad_out_bias,
        ]
    )
    grad_normed = jnp.einsum(
        "te,de->td", grad_mixed, qkv_weight, preferred_element_type=jnp.float32
    )
    grad_in_part, gain_one, shift_one = norm_back(
        plain_in, norm_gains[0], norm_shifts[0], grad_normed
    )
    input_grad = (
        (grad_middle + grad_in_part).astype(jnp.bfloat16).reshape(1, row_count, length, model_width)
    )
    grad_gain = jnp.stack([gain_one, gain_two])
    grad_shift = jnp.stack([shift_one, shift_two])
    grad_dist = jnp.sum(grad_table, axis=0).T
    everything = lax.psum(
        (
            grad_gain,
            grad_shift,
            grad_qkv,
            grad_bias_rows,
            grad_dist,
            grad_out,
            ffn_sums[0],
            ffn_sums[1],
            ffn_sums[2],
            ffn_sums[3],
        ),
        "batch",
    )
    (
        sum_gain,
        sum_shift,
        sum_qkv,
        sum_bias,
        sum_dist,
        sum_out,
        sum_up,
        sum_down,
        sum_up_bias,
        sum_down_bias,
    ) = everything
    return (
        output,
        input_grad,
        sum_gain[None],
        sum_shift[None],
        sum_qkv[None],
        sum_bias[None],
        sum_dist[None],
        sum_out[None],
        sum_up[None],
        sum_up_bias[None],
        sum_down[None],
        sum_down_bias[None],
    )


def solution(mesh):
    in_specs = (
        P("stream", "batch", None, None),
        P("stream", "batch", None, None),
        P("batch", None),
        P("stream", "batch", None, None),
        P("stream", None, None),
        P("stream", None, None),
        P("stream", None, None),
        P("stream", None, None),
        P("stream", None, None),
        P("stream", None, None),
        P("stream", None, None),
        P("stream", None),
        P("stream", None, None),
        P("stream", None),
    )
    out_specs = (
        P("stream", "batch", None, None),
        P("stream", "batch", None, None),
        P("stream", None, None),
        P("stream", None, None),
        P("stream", None, None),
        P("stream", None, None),
        P("stream", None, None),
        P("stream", None, None),
        P("stream", None, None),
        P("stream", None),
        P("stream", None, None),
        P("stream", None),
    )
    return jax.shard_map(
        on_device, mesh=mesh, in_specs=in_specs, out_specs=out_specs, check_vma=False
    )
```

profile of v0, /device:TPU:0, one launch (start us, length us, event | category | flops | bytes accessed | tf_op | source)
XLA Modules:
  0.0 1398.9 jit_solution(17615919433728705814)
XLA Ops:
  13.2 3.8 fusion.43
  34.5 58.0 %collective-permute-done = bf16[2,1024,768]{2,1,0:T(8,128)(2,1)} collective-permute-done((bf16[2,1024,768]{2,1,0:T(8,128)(2,1)}, bf16[2,1024,768]{2,1,0:T(8,128)(2,1)}, u32[]{:S(2)}, u32[]{:S(2)}) %collective-permute-start) | collective-permute-done | bytes 3145760 | tf_op jit(solution)/shard_map/ppermute | solution.py:20
  92.5 3.7 fusion.84
  101.4 197.8 %while.28 = (s32[]{:T(128)}, bf16[2,512,768]{2,1,0:T(8,128)(2,1)}, f32[2,12,512]{2,1,0:T(8,128)}, bf16[2,512,768]{1,2,0:T(8,128)(2,1)}, bf16[2,512,768]{1,2,0:T(...) while((s32[]{:T(128)}, bf16[2,512,768]{2,1,0:T(8,128)(2,1)}, ...), condition=%wide.region_5.6_spmd, body=%wide.region_2.5_spmd.sunk | while | flops 2498619392 | bytes 255981456 | solution.py:147
  102.4 13.4 convolution_bitcast_fusion.8
  115.9 11.3 slice_add_fusion.6
  127.2 19.1 %copy.105 = f32[2,8,512,512]{3,2,1,0:T(8,128)} copy(f32[2,8,512,512]{3,1,2,0:T(8,128)S(1)} %bitcast.298) | data formatting | bytes 33554432 | tf_op jit(solution)/shard_map/while
  147.3 11.0 slice_select_fusion.4
  160.5 13.0 fusion.130
  173.5 11.0 fusion.131
  184.6 11.3 fusion.132
  201.1 13.4 convolution_bitcast_fusion.8
  214.6 11.3 slice_add_fusion.6
  225.9 19.1 %copy.105 = f32[2,8,512,512]{3,2,1,0:T(8,128)} copy(f32[2,8,512,512]{3,1,2,0:T(8,128)S(1)} %bitcast.298) | data formatting | bytes 33554432 | tf_op jit(solution)/shard_map/while
  245.9 11.0 slice_select_fusion.4
  259.2 13.0 fusion.130
  272.2 11.0 fusion.131
  283.3 11.3 fusion.132
  299.2 3.9 fusion.85
  304.0 35.3 %multiply_convert_fusion.1 = (bf16[1024,3072]{1,0:T(8,128)(2,1)}, f32[1024,3072]{1,0:T(8,128)}, f32[1024,3072]{1,0:T(8,128)}) fusion(f32[3072]{0:T(1024)S(1)} %bitcast.368, bf16[1,768,3072]{2,1,0:T(8,128)(2,1)S(1)} %bitcast.364, f32[1024,768]{1,0:T(8,128)S(1)} %get-tuple-element.341, f32[768]{0:T(1024)S(1)} %copy-done.44, f32[768]{0:T(1024)S(1)} %copy-done.38, ...), kind=kOutput, calls=%fused_computation.74 | convolution fusion | flops 5043388416 | bytes 39348224 | tf_op jit(solution)/shard_map/dot_general | solution.py:164
  339.3 17.0 %convert_reduce_fusion = (f32[3072]{0:T(1024)}, bf16[1024,3072]{1,0:T(8,128)(2,1)}) fusion(f32[1024,3072]{1,0:T(8,128)} %get-tuple-element.307, bf16[1024,768]{1,0:T(8,128)(2,1)} %bitcast.328, bf16[1,3072,768]{2,1,0:T(8,128)(2,1)} %param.30, f32[1024,3072]{1,0:T(8,128)} %get-tuple-element.342, f32[3072]{0:T(1024)} %bitcast.367), kind=kOutput, calls=%fused_computation.72 | convolution fusion | flops 4885312512 | bytes 37773312 | tf_op jit(solution)/shard_map/td,fd->tf/dot_general | solution.py:174
  356.3 10.2 multiply_reduce_fusion.1
  372.8 409.8 %while.29 = (s32[]{:T(128)}, bf16[2,512,768]{2,1,0:T(8,128)(2,1)}, f32[2,1024,768]{2,1,0:T(8,128)}, f32[2,1024,768]{2,1,0:T(8,128)}, f32[2,12,64]{2,1,0:T(8,128)...) while((s32[]{:T(128)}, bf16[2,512,768]{2,1,0:T(8,128)(2,1)}, ...), condition=%wide.region_12.13_spmd, body=%wide.region_10.12_spmd.sunk | while | flops 5344585728 | bytes 571104000 | solution.py:248
  395.7 13.4 convolution_bitcast_fusion.9
  409.1 11.3 slice_add_fusion.7
  420.4 19.1 %copy.109 = f32[2,8,512,512]{3,2,1,0:T(8,128)} copy(f32[2,8,512,512]{3,1,2,0:T(8,128)S(1)} %bitcast.299) | data formatting | bytes 33554432 | tf_op jit(solution)/shard_map/while
  439.8 10.9 slice_select_fusion.5
  457.6 13.0 fusion.143
  472.4 20.8 %multiply_reduce_fusion.5 = (f32[12,512]{1,0:T(8,128)S(1)}, f32[12,512,1024]{2,1,0:T(8,128)}) fusion(f32[12,512,1024]{2,1,0:T(8,128)} %fusion.143, f32[12,512]{1,0:T(8,128)S(1)} %dynamic-slice_bitcast_fusion.2, f32[12,512,512]{2,1,0:T(8,128)S(1)} %bitcast.303, bf16[512,12,64]{0,2,1:T(8,128)(2,1)S(1)} %bitcast.309, ...), kind=kOutput, calls=%fused_computation.37.clone.1 | convolution fusion | flops 839903232 | bytes 65323008 | tf_op jit(solution)/shard_map/while/body/eval_jaxpr/qhd,khd->hqk/dot_general | solution.py:75
  493.2 16.1 %multiply_convert_fusion.3 = bf16[12,512,1024]{2,1,0:T(8,128)(2,1)S(1)} fusion(f32[12,512,1024]{2,1,0:T(8,128)} %get-tuple-element.543, f32[12,512,1024]{2,1,0:T(8,128)} %fusion.143, f32[12,512]{1,0:T(8,128)S(1)} %get-tuple-element.544), kind=kLoop, calls=%fused_computation.36.clone.1 | loop fusion | flops 18874368 | bytes 62939136 | tf_op jit(solution)/shard_map/while/body/eval_jaxpr/convert_element_type | solution.py:219
  509.3 4.6 convolution_multiply_fusion.5
  518.3 12.4 fusion.144
  530.7 3.5 copy.111
  534.2 5.9 constant_dynamic-update-slice_fusion.9
  543.0 4.1 pad.118
  547.1 11.6 copy.113
  558.7 12.0 fusion.145
  570.7 9.4 convolution_multiply_fusion.4
  585.4 13.4 convolution_bitcast_fusion.9
  598.8 11.3 slice_add_fusion.7
  610.1 19.1 %copy.109 = f32[2,8,512,512]{3,2,1,0:T(8,128)} copy(f32[2,8,512,512]{3,1,2,0:T(8,128)S(1)} %bitcast.299) | data formatting | bytes 33554432 | tf_op jit(solution)/shard_map/while
  629.5 10.9 slice_select_fusion.5
  647.3 13.0 fusion.143
  662.1 20.8 %multiply_reduce_fusion.5 = (f32[12,512]{1,0:T(8,128)S(1)}, f32[12,512,1024]{2,1,0:T(8,128)}) fusion(f32[12,512,1024]{2,1,0:T(8,128)} %fusion.143, f32[12,512]{1,0:T(8,128)S(1)} %dynamic-slice_bitcast_fusion.2, f32[12,512,512]{2,1,0:T(8,128)S(1)} %bitcast.303, bf16[512,12,64]{0,2,1:T(8,128)(2,1)S(1)} %bitcast.309, ...), kind=kOutput, calls=%fused_computation.37.clone.1 | convolution fusion | flops 839903232 | bytes 65323008 | tf_op jit(solution)/shard_map/while/body/eval_jaxpr/qhd,khd->hqk/dot_general | solution.py:75
  682.9 16.1 %multiply_convert_fusion.3 = bf16[12,512,1024]{2,1,0:T(8,128)(2,1)S(1)} fusion(f32[12,512,1024]{2,1,0:T(8,128)} %get-tuple-element.543, f32[12,512,1024]{2,1,0:T(8,128)} %fusion.143, f32[12,512]{1,0:T(8,128)S(1)} %get-tuple-element.544), kind=kLoop, calls=%fused_computation.36.clone.1 | loop fusion | flops 18874368 | bytes 62939136 | tf_op jit(solution)/shard_map/while/body/eval_jaxpr/convert_element_type | solution.py:219
  699.0 4.6 convolution_multiply_fusion.5
  708.0 12.4 fusion.144
  720.4 3.5 copy.111
  723.9 5.9 constant_dynamic-update-slice_fusion.9
  732.7 4.1 pad.118
  736.8 11.6 copy.113
  748.4 12.0 fusion.145
  760.4 9.4 convolution_multiply_fusion.4
  793.0 8.3 convolution_bitcast_fusion.3
  801.3 10.1 convolution_bitcast_fusion.2
  811.4 49.1 %collective-permute-done.1 = bf16[2,1024,768]{2,1,0:T(8,128)(2,1)S(1)} collective-permute-done((bf16[2,1024,768]{2,1,0:T(8,128)(2,1)S(1)}, bf16[2,1024,768]{2,1,0:T(8,128)(2,1)S(1)}, u32[]{:S(2)}, u32[]{:S(2)}) %collective-permute-start.1) | collective-permute-done | bytes 3145760 | tf_op jit(solution)/shard_map/ppermute | solution.py:20
  864.1 6.1 fusion.79
  875.2 6.3 convolution_bitcast_fusion.4
  891.9 10.0 add_convert_fusion.3
  903.2 64.7 %all-reduce.2 = (f32[1,2,768]{2,1,0:T(2,128)}, f32[1,2,768]{2,1,0:T(2,128)}, f32[1,3,768]{2,0,1:T(1,128)}, f32[1,64,12]{1,0,2:T(1,128)}, f32[1,3072]{1,0:T(1,128)}, /*index=5*/f32[1,768]{1,0:T(1,128)}) all-reduce(f32[1,2,768]{2,1,0:T(2,128)} %maximum_bitcast_fusion.1, ...), channel_id=1, replica_groups=mesh['stream'=2,'batch'=16] {'batch'}, use_global_device_ids=true, to_apply=%region_17.18 | all-reduce | flops 9984 | bytes 79872 | tf_op jit(solution)/shard_map/psum | solution.py:297
  967.9 402.9 %all-reduce.6.cloned.1.call-done = (f32[1,768,2304]{2,1,0:T(8,128)}, f32[1,768,768]{2,1,0:T(8,128)}, f32[1,768,3072]{2,1,0:T(8,128)}, f32[1,3072,768]{2,1,0:T(8,128)}) async-done(((f32[1,768,2304]{2,1,0:T(8,128)}, f32[1,768,768]{2,1,0:T(8,128)}, f32[1,768,3072]{2,1,0:T(8,128)}, f32[1,3072,768]{2,1,0:T(8,128)}), (f32[1,768,2304]{2,1,0:T(8,128)}, f32[1,768,768]{2,1,0:T(8,128)}, f32[1,768,3072]{2,1,0:T(8,128)}, ...) | async-done | bytes 28311568 | tf_op jit(solution)/shard_map/psum | solution.py:297
  1370.8 6.6 copy.148
  1378.8 9.3 copy.150
  1388.1 3.7 copy.151
  (341 shorter events, 126.5 us)
Async XLA Ops:
  7.2 6.0 copy-start
  7.2 1363.6 %all-reduce.6.cloned.1.call-start = ((), (), s32[]{:S(2)}) async-start(), calls=%async_computation | async-start | bytes 56623104 | tf_op jit(solution)/shard_map/psum | solution.py:297
  7.3 5.2 copy-start.16
  21.1 71.4 %collective-permute-start = (bf16[2,1024,768]{2,1,0:T(8,128)(2,1)}, bf16[2,1024,768]{2,1,0:T(8,128)(2,1)}, u32[]{:S(2)}, u32[]{:S(2)}) collective-permute-start(bf16[2,1024,768]{2,1,0:T(8,128)(2,1)} %pad_maximum_fusion.4), channel_id=1, source_target_pairs={{0,16},{16,0},{1,17},{17,1},{2,18},{18,2},{3,19},{19,3},{4,20},{20... | collective-permute-start | bytes 9437192 | tf_op jit(solution)/shard_map/ppermute | solution.py:20
  28.0 6.5 copy-start.62
  127.2 19.1 %copy-start.40 = (s32[2,512]{1,0:T(2,128)S(1)}, s32[2,512]{1,0:T(2,128)}, u32[]{:S(2)}) copy-start(s32[2,512]{1,0:T(2,128)} %get-tuple-element.585) | copy-start | bytes 12292 | tf_op jit(solution)/shard_map/while
  147.2 11.1 copy-start.10
  173.5 11.0 copy-start.30
  173.5 11.1 copy-start.9
  184.5 11.4 copy-start.31
  225.9 19.1 %copy-start.40 = (s32[2,512]{1,0:T(2,128)S(1)}, s32[2,512]{1,0:T(2,128)}, u32[]{:S(2)}) copy-start(s32[2,512]{1,0:T(2,128)} %get-tuple-element.585) | copy-start | bytes 12292 | tf_op jit(solution)/shard_map/while
  245.9 11.1 copy-start.10
  272.2 11.0 copy-start.30
  272.2 11.1 copy-start.9
  283.2 11.4 copy-start.31
  303.2 63.3 %copy-start.18 = (f32[1024,768]{1,0:T(8,128)}, f32[1024,768]{1,0:T(8,128)S(1)}, u32[]{:S(2)}) copy-start(f32[1024,768]{1,0:T(8,128)S(1)} %get-tuple-element.341) | copy-start | bytes 9437188
  303.2 63.3 %copy-start.33 = (f32[1024]{0:T(1024)}, f32[1024]{0:T(1024)S(1)}, u32[]{:S(2)}) copy-start(f32[1024]{0:T(1024)S(1)} %broadcast_multiply_fusion) | copy-start | bytes 12292
  303.8 62.7 %copy-start.35 = (f32[1024]{0:T(1024)}, f32[1024]{0:T(1024)S(1)}, u32[]{:S(2)}) copy-start(f32[1024]{0:T(1024)S(1)} %fusion.72) | copy-start | bytes 12292
  395.6 13.4 copy-start.7
  420.4 19.1 %copy-start.41 = (s32[2,512]{1,0:T(2,128)S(1)}, s32[2,512]{1,0:T(2,128)}, u32[]{:S(2)}) copy-start(s32[2,512]{1,0:T(2,128)} %get-tuple-element.640) | copy-start | bytes 12292 | tf_op jit(solution)/shard_map/while
  457.5 14.9 %slice-start.1 = ((s8[12582912]{0:T(1024)(128)(4,1)}), s8[4194304]{0:T(1024)(128)(4,1)S(1)}, s32[]{:S(2)}) async-start(s8[12582912]{0:T(1024)(128)(4,1)} %bitcast.302), calls=%async_computation.2 | async-start | bytes 8388608 | tf_op jit(solution)/shard_map/while
  457.5 13.1 copy-start.11
  457.5 13.1 copy-start.15
  457.5 14.9 %slice-start.2 = ((s8[12582912]{0:T(1024)(128)(4,1)}), s8[4194304]{0:T(1024)(128)(4,1)S(1)}, s32[]{:S(2)}) async-start(s8[12582912]{0:T(1024)(128)(4,1)} %bitcast.302), calls=%async_computation.3 | async-start | bytes 8388608 | tf_op jit(solution)/shard_map/while
  457.5 14.9 %slice-start.3 = ((s8[12582912]{0:T(1024)(128)(4,1)}), s8[4194304]{0:T(1024)(128)(4,1)S(1)}, s32[]{:S(2)}) async-start(s8[12582912]{0:T(1024)(128)(4,1)} %bitcast.302), calls=%async_computation.4 | async-start | bytes 8388608 | tf_op jit(solution)/shard_map/while
  470.7 22.4 %copy-start.3 = (bf16[1,512,768]{1,2,0:T(8,128)(2,1)}, bf16[1,512,768]{1,2,0:T(8,128)(2,1)S(1)}, u32[]{:S(2)}) copy-start(bf16[1,512,768]{1,2,0:T(8,128)(2,1)S(1)} %constant_dynamic-slice_fusion.41) | copy-start | bytes 2359300 | tf_op jit(solution)/shard_map/while
  472.4 20.8 %copy-start.5 = (bf16[1,512,768]{1,2,0:T(8,128)(2,1)}, bf16[1,512,768]{1,2,0:T(8,128)(2,1)S(1)}, u32[]{:S(2)}) copy-start(bf16[1,512,768]{1,2,0:T(8,128)(2,1)S(1)} %constant_dynamic-slice_fusion.42) | copy-start | bytes 2359300 | tf_op jit(solution)/shard_map/while
  509.3 5.4 copy-start.1
  547.0 11.6 copy-start.8
  547.0 11.6 copy-start.52
  558.7 12.1 copy-start.4
  558.7 12.1 copy-start.6
  570.7 9.4 copy-start.53
  585.3 13.4 copy-start.7
  610.1 19.1 %copy-start.41 = (s32[2,512]{1,0:T(2,128)S(1)}, s32[2,512]{1,0:T(2,128)}, u32[]{:S(2)}) copy-start(s32[2,512]{1,0:T(2,128)} %get-tuple-element.640) | copy-start | bytes 12292 | tf_op jit(solution)/shard_map/while
  647.2 14.9 %slice-start.1 = ((s8[12582912]{0:T(1024)(128)(4,1)}), s8[4194304]{0:T(1024)(128)(4,1)S(1)}, s32[]{:S(2)}) async-start(s8[12582912]{0:T(1024)(128)(4,1)} %bitcast.302), calls=%async_computation.2 | async-start | bytes 8388608 | tf_op jit(solution)/shard_map/while
  647.2 13.1 copy-start.11
  647.2 13.1 copy-start.15
  647.2 14.9 %slice-start.2 = ((s8[12582912]{0:T(1024)(128)(4,1)}), s8[4194304]{0:T(1024)(128)(4,1)S(1)}, s32[]{:S(2)}) async-start(s8[12582912]{0:T(1024)(128)(4,1)} %bitcast.302), calls=%async_computation.3 | async-start | bytes 8388608 | tf_op jit(solution)/shard_map/while
  647.2 14.9 %slice-start.3 = ((s8[12582912]{0:T(1024)(128)(4,1)}), s8[4194304]{0:T(1024)(128)(4,1)S(1)}, s32[]{:S(2)}) async-start(s8[12582912]{0:T(1024)(128)(4,1)} %bitcast.302), calls=%async_computation.4 | async-start | bytes 8388608 | tf_op jit(solution)/shard_map/while
  660.4 22.4 %copy-start.3 = (bf16[1,512,768]{1,2,0:T(8,128)(2,1)}, bf16[1,512,768]{1,2,0:T(8,128)(2,1)S(1)}, u32[]{:S(2)}) copy-start(bf16[1,512,768]{1,2,0:T(8,128)(2,1)S(1)} %constant_dynamic-slice_fusion.41) | copy-start | bytes 2359300 | tf_op jit(solution)/shard_map/while
  662.1 20.8 %copy-start.5 = (bf16[1,512,768]{1,2,0:T(8,128)(2,1)}, bf16[1,512,768]{1,2,0:T(8,128)(2,1)S(1)}, u32[]{:S(2)}) copy-start(bf16[1,512,768]{1,2,0:T(8,128)(2,1)S(1)} %constant_dynamic-slice_fusion.42) | copy-start | bytes 2359300 | tf_op jit(solution)/shard_map/while
  699.0 5.4 copy-start.1
  736.7 11.6 copy-start.8
  736.8 11.6 copy-start.52
  748.4 12.1 copy-start.4
  748.4 12.1 copy-start.6
  760.4 9.4 copy-start.53
  782.6 8.0 slice-start.9
  784.8 5.8 slice-start.10
  784.8 8.1 slice-start.7
  791.1 10.2 copy-start.23
  791.1 69.4 %collective-permute-start.1 = (bf16[2,1024,768]{2,1,0:T(8,128)(2,1)S(1)}, bf16[2,1024,768]{2,1,0:T(8,128)(2,1)S(1)}, u32[]{:S(2)}, u32[]{:S(2)}) collective-permute-start(bf16[2,1024,768]{2,1,0:T(8,128)(2,1)S(1)} %pad_maximum_fusion.5), channel_id=1, source_target_pairs={{0,16},{16,0},{1,17},{17,1},{2,18},{18,2},{3,19},{19,3},{4,20},{20... | collective-permute-start | bytes 9437192 | tf_op jit(solution)/shard_map/ppermute | solution.py:20
  864.1 6.1 copy-start.54
  881.5 5.9 copy-start.51
  891.8 10.1 copy-start.57
  891.8 10.1 copy-start.58
  891.9 10.1 copy-start.63
  891.9 10.2 copy-start.55
  891.9 10.8 copy-start.56
  1370.8 6.6 copy-start.25
  1377.3 10.7 slice-start.4
  1378.8 9.3 slice-start.5
  1378.8 9.3 slice-start.6
  (45 other events, 112.5 us)
Sparse Core Ops, SparseCore 0:
  881.6 489.0 all-reduce.5
where the time goes:
time: 1410 us; the launch traced here: 1400 us
  waiting for transfers between devices  510 us (36%)
  matrix products  363 us (26%)
  local copies, waits for them, and re-layouts  235 us (17%)
  other arithmetic  175 us (12%)
  blocking collectives  64.7 us (5%)
  loops' own time  31.4 us (2%)
  between operations  14.9 us (1%)
    psum x1, waiting for transfers between devices, on_device(): lax.psum((grad_gain, grad_shift, grad_qkv, grad_bias_rows, grad_dist, gra...  403 us
    while x112, local copies, waits for them, and re-layouts  115 us
    ppermute x2, waiting for transfers between devices, from_partner(): return lax.ppermute(block, axis, route)  107 us
    dot_general x4, matrix products, score_block(): jnp.einsum('qhd,khd->hqk', split_heads(queries, heads_count), split_heads...  67.5 us
    psum x1, blocking collectives, on_device(): lax.psum((grad_gain, grad_shift, grad_qkv, grad_bias_rows, grad_dist, gra...  64.7 us
    dot_general x4, matrix products, bias_block(): jnp.dot(table_parts, onehot, preferred_element_type=jnp.float32)  53.7 us
    add x4, other arithmetic, bias_block(): looked_both[:heads_count] + looked_both[heads_count:]  45.2 us
    select_n x4, other arithmetic, bias_block(): masked_bias = jnp.where(allowed[None], looked, MASKED)  43.9 us
  transfers between devices with their start and end apart: 3, of which 3 were waited for; matrix products, arithmetic and copies ran while one was open for 4% of the time, Pallas kernels for 0%

commit v1 on v0

v1 whole, which is shorter than its diff:
```python
import functools
import jax
import jax.numpy as jnp
from jax import lax
from jax.experimental import pallas as pl
from jax.experimental.pallas import tpu as pltpu
from jax.sharding import PartitionSpec as P

GRID = 8
EPSILON = 1e-05
MASKED = -1000000000.0

NT=(((1,),(1,)),((),())); NN=(((1,),(0,)),((),())); TN=(((0,),(0,)),((),()))
def mm(a,b,dn=NN): return lax.dot_general(a,b,dn,preferred_element_type=jnp.float32)
BF=jnp.bfloat16

def three(x):
    hi=x.astype(BF); r=x-hi.astype(jnp.float32); mid=r.astype(BF); lo=(r-mid.astype(jnp.float32)).astype(BF)
    return hi,mid,lo

def fwd_kernel(CQ, q_ref,kn_ref,kf_ref,vn_ref,vf_ref,e_ref,b_ref,qseg_ref,kseg_ref,o_ref,qm_ref):
    pair=pl.program_id(1)
    L=q_ref.shape[0]
    lane=lax.broadcasted_iota(jnp.int32,(1,128),1)
    @pl.when(pair==0)
    def _():
        qm_ref[...]=qseg_ref[...]
    outs=[None]*(L//CQ)
    for hh in range(2):
        mh=(lane<64) if hh==0 else (lane>=64)
        h=2*pair+hh
        C=mm(e_ref[...],b_ref[hh]).astype(BF)
        kx=jnp.concatenate([kn_ref[...],C,kseg_ref[...]],axis=1)
        kf=kf_ref[...]
        one=jnp.ones((),BF); zero=jnp.zeros((),BF)
        vnx=jnp.where(mh,vn_ref[...],one); vfx=jnp.where(mh,vf_ref[...],one)
        for c in range(L//CQ):
            sl=slice(c*CQ,(c+1)*CQ)
            qm=jnp.where(mh,q_ref[sl,:],zero)
            qx=jnp.concatenate([qm,e_ref[sl,:],qseg_ref[sl,:]],axis=1)
            sn=mm(qx,kx,NT); sf=mm(qm,kf,NT)
            m=jnp.maximum(jnp.max(sn,axis=1,keepdims=True),jnp.max(sf,axis=1,keepdims=True))
            pn=jnp.exp(sn-m).astype(BF); pf=jnp.exp(sf-m).astype(BF)
            o=mm(pn,vnx)+mm(pf,vfx)
            l=pltpu.roll(o,64,1)
            on=o/l
            outs[c]=on if hh==0 else jnp.where(mh,on,outs[c])
            lse=-(m+jnp.log(jnp.where(mh,l,o)))
            hi,mid,lo=three(lse)
            cur=qm_ref[sl,:]
            cur=jnp.where(lane==3*h,hi,cur); cur=jnp.where(lane==3*h+1,mid,cur); cur=jnp.where(lane==3*h+2,lo,cur)
            qm_ref[sl,:]=cur
    for c in range(L//CQ):
        o_ref[c*CQ:(c+1)*CQ,:]=outs[c].astype(BF)

def fwd(q,kn,kf,vn,vf,e,bt,qseg,kseg,L,CQ=512):
    T=q.shape[0]; R=T//L; NP=q.shape[1]//128
    blk=pl.BlockSpec((L,128),lambda r,p:(r,p))
    row=lambda w: pl.BlockSpec((L,w),lambda r,p:(r,0))
    return pl.pallas_call(functools.partial(fwd_kernel,CQ),grid=(R,NP),
        in_specs=[blk]*5+[row(256),pl.BlockSpec((2,256,256),lambda r,p:(p,0,0)),row(128),row(128)],
        out_specs=[blk,row(128)],
        out_shape=[jax.ShapeDtypeStruct(q.shape,BF),jax.ShapeDtypeStruct((T,128),BF)],
        compiler_params=pltpu.CompilerParams(vmem_limit_bytes=48<<20),name="att_fwd")(q,kn,kf,vn,vf,e,bt,qseg,kseg)

def bwd_kernel(CK,MODE, q_ref,kn_ref,kf_ref,vn_ref,vf_ref,do_ref,o_ref,e_ref,et_ref,b_ref,qmisc_ref,kseg_ref,
               dq_ref,dkn_ref,dkf_ref,dvn_ref,dvf_ref,g_ref):
    pair=pl.program_id(0); r=pl.program_id(1)
    L=q_ref.shape[0]
    lane=lax.broadcasted_iota(jnp.int32,(1,128),1)
    zero=jnp.zeros((),BF)
    n=L//CK
    dkn=[None]*n; dkf=[None]*n; dvn=[None]*n; dvf=[None]*n
    dq=None
    prod=do_ref[...].astype(jnp.float32)*o_ref[...].astype(jnp.float32)
    add=lambda a,b: b if a is None else a+b
    for hh in range(2):
        mh=(lane<64) if hh==0 else (lane>=64)
        h=2*pair+hh
        delta=-jnp.sum(jnp.where(mh,prod,0.0),axis=1,keepdims=True)
        hi,mid,lo=three(delta)
        dmisc=jnp.where(lane==0,hi,jnp.where(lane==1,mid,zero))
        qm=jnp.where(mh,q_ref[...],zero); dom=jnp.where(mh,do_ref[...],zero)
        C=mm(e_ref[...],b_ref[hh]).astype(BF)
        ones_h=jnp.where((lane>=3*h)&(lane<3*h+3),1.0,0.0)
        ones_b=jnp.broadcast_to(ones_h.astype(BF),(CK,128))
        ones01=jnp.broadcast_to(jnp.where(lane<2,1.0,0.0).astype(BF),(CK,128))
        qx=jnp.concatenate([qm,e_ref[...],qmisc_ref[...]],axis=1)
        qf=jnp.concatenate([qm,qmisc_ref[...]],axis=1)
        dox=jnp.concatenate([dom,dmisc],axis=1)
        qe=jnp.concatenate([qm,e_ref[...]],axis=1)
        g=None
        for c in range(n):
            sl=slice(c*CK,(c+1)*CK)
            kseg=(kseg_ref[sl,:].astype(jnp.float32)+ones_h).astype(BF)
            kx=jnp.concatenate([kn_ref[sl,:],C[sl,:],kseg],axis=1)
            p=jnp.exp(mm(kx,qx,NT))
            vx=jnp.concatenate([vn_ref[sl,:],ones01],axis=1)
            ds=(p*mm(vx,dox,NT)).astype(BF); pb=p.astype(BF)
            dvn[c]=add(dvn[c],mm(pb,dom))
            t=mm(ds,qe)
            dkn[c]=add(dkn[c],t[:,:128])
            g=add(g,mm(et_ref[:,sl],t[:,128:].astype(BF)))
            dq=add(dq,mm(ds,jnp.where(mh,kn_ref[sl,:],zero),TN))
        for c in range(n):
            sl=slice(c*CK,(c+1)*CK)
            kx=jnp.concatenate([kf_ref[sl,:],ones_b],axis=1)
            p=jnp.exp(mm(kx,qf,NT))
            vx=jnp.concatenate([vf_ref[sl,:],ones01],axis=1)
            ds=(p*mm(vx,dox,NT)).astype(BF); pb=p.astype(BF)
            dvf[c]=add(dvf[c],mm(pb,dom))
            dkf[c]=add(dkf[c],mm(ds,qm))
            dq=add(dq,mm(ds,jnp.where(mh,kf_ref[sl,:],zero),TN))
        @pl.when(r==0)
        def _(): g_ref[hh]=g
        @pl.when(r!=0)
        def _(): g_ref[hh]+=g
    dq_ref[...]=(dq*0.125).astype(BF)
    for c in range(n):
        sl=slice(c*CK,(c+1)*CK)
        dkn_ref[sl,:]=dkn[c].astype(BF); dkf_ref[sl,:]=dkf[c].astype(BF)
        dvn_ref[sl,:]=dvn[c].astype(BF); dvf_ref[sl,:]=dvf[c].astype(BF)

def bwd(q,kn,kf,vn,vf,do,o,e,et,bt,qmisc,kseg,L,CK=512,MODE=0):
    T=q.shape[0]; R=T//L; NP=q.shape[1]//128
    blk=pl.BlockSpec((L,128),lambda p,r:(r,p))
    row=lambda w: pl.BlockSpec((L,w),lambda p,r:(r,0))
    return pl.pallas_call(functools.partial(bwd_kernel,CK,MODE),grid=(NP,R),
        in_specs=[blk]*7+[row(256),pl.BlockSpec((256,L),lambda p,r:(0,r)),pl.BlockSpec((2,256,256),lambda p,r:(p,0,0)),row(128),row(128)],
        out_specs=[blk]*5+[pl.BlockSpec((2,256,256),lambda p,r:(p,0,0))],
        out_shape=[jax.ShapeDtypeStruct(q.shape,BF)]*5+[jax.ShapeDtypeStruct((2*NP,256,256),jnp.float32)],
        compiler_params=pltpu.CompilerParams(vmem_limit_bytes=48<<20),name="att_bwd")(q,kn,kf,vn,vf,do,o,e,et,bt,qmisc,kseg)


def from_partner(block, axis, stride):
    count = lax.axis_size(axis)
    route = []
    for low in range(count):
        high = low | 1 << stride
        if high != low and high < count:
            route += [(low, high), (high, low)]
    return lax.ppermute(block, axis, route)


def layer_norm(values, norm_gain, norm_shift):
    center = values - jnp.mean(values, axis=-1, keepdims=True)
    spread = jnp.mean(center * center, axis=-1, keepdims=True)
    return center * lax.rsqrt(spread + EPSILON) * norm_gain + norm_shift


def norm_back(values, norm_gain, norm_shift, upstream):
    unused, pull_back = jax.vjp(layer_norm, values, norm_gain, norm_shift)
    return pull_back(upstream)


def gelu_exact(values):
    return jax.nn.gelu(values, approximate=False)


def gelu_back(values, upstream):
    unused, pull_back = jax.vjp(gelu_exact, values)
    return pull_back(upstream)[0]


def prepare(segment_ids, box_cells, table, is_vision):
    cell = (box_cells[:, 0] * 16 + box_cells[:, 1]).reshape(-1)
    cells = jnp.arange(256)
    e = (cell[:, None] == cells[None]).astype(BF)
    et = (cells[:, None] == cell[None]).astype(BF)
    lane = jnp.arange(128)
    same = segment_ids.reshape(-1)[:, None] == lane[None] - 64
    inside = (lane >= 64) & (lane < 68)
    qseg = same.astype(BF)
    kseg = jnp.where(inside[None] & ~same & jnp.logical_not(is_vision), MASKED, 0.0).astype(BF)
    return e, et, qseg, kseg


def code_onehot():
    c = jnp.arange(65536)
    step_x = jnp.minimum(jnp.abs(c // 4096 - (c // 16) % 16), GRID - 1)
    step_y = jnp.minimum(jnp.abs((c // 256) % 16 - c % 16), GRID - 1)
    return ((step_x * GRID + step_y)[None] == jnp.arange(GRID * GRID)[:, None]).astype(BF)


def on_device(features, cotangent, segment_ids, box_cells, ln_gain, ln_shift, w_qkv, attn_bias,
              distance_table, w_out, w_up, up_bias, w_down, down_bias):
    rows, length, width = features.shape[1:]
    tokens = rows * length
    heads = distance_table.shape[2]
    is_vision = lax.axis_index("stream") != 0
    norm_gains, norm_shifts = ln_gain[0], ln_shift[0]
    bias_rows = attn_bias[0]
    qkv_weight, out_weight, up_weight, down_weight = w_qkv[0], w_out[0], w_up[0], w_down[0]
    plain_in = features[0].reshape(tokens, width).astype(jnp.float32)
    normed = layer_norm(plain_in, norm_gains[0], norm_shifts[0]).astype(BF)
    combined = jnp.dot(normed, qkv_weight, preferred_element_type=jnp.float32)
    queries = (combined[:, :width] + bias_rows[0]).astype(BF) * BF(0.125)
    key_part = combined[:, width:2 * width].astype(BF)
    value_part = (combined[:, 2 * width:] + bias_rows[1]).astype(BF)
    partner_k = from_partner(key_part, "stream", 0)
    partner_v = from_partner(value_part, "stream", 0)
    e, et, qseg, kseg = prepare(segment_ids, box_cells[0], distance_table[0], is_vision)
    onehot = code_onehot()
    bt = jnp.dot(distance_table[0].T.astype(BF), onehot, preferred_element_type=jnp.float32).astype(BF).reshape(heads, 256, 256)
    attended, qmisc = fwd(queries, key_part, partner_k, value_part, partner_v, e, bt, qseg, kseg, length)
    middle = plain_in + jnp.dot(attended, out_weight, preferred_element_type=jnp.float32) + bias_rows[2]
    normed_two = layer_norm(middle, norm_gains[1], norm_shifts[1]).astype(BF)
    pre_act = jnp.dot(normed_two, up_weight, preferred_element_type=jnp.float32) + up_bias[0]
    activated = gelu_exact(pre_act).astype(BF)
    result = middle + jnp.dot(activated, down_weight, preferred_element_type=jnp.float32) + down_bias[0]
    output = result.astype(BF).reshape(1, rows, length, width)
    cot_bf = cotangent[0].reshape(tokens, width)
    cot_f32 = cot_bf.astype(jnp.float32)
    grad_down = jnp.einsum("tf,td->fd", activated, cot_bf, preferred_element_type=jnp.float32).astype(BF)
    grad_down_bias = jnp.sum(cot_f32, axis=0)
    grad_act = jnp.einsum("td,fd->tf", cot_bf, down_weight, preferred_element_type=jnp.float32)
    grad_pre = gelu_back(pre_act, grad_act).astype(BF)
    grad_up = jnp.einsum("td,tf->df", normed_two, grad_pre, preferred_element_type=jnp.float32).astype(BF)
    grad_up_bias = jnp.sum(grad_pre.astype(jnp.float32), axis=0)
    grad_normed_two = jnp.einsum("tf,df->td", grad_pre, up_weight, preferred_element_type=jnp.float32)
    grad_mid_part, gain_two, shift_two = norm_back(middle, norm_gains[1], norm_shifts[1], grad_normed_two)
    grad_middle = cot_f32 + grad_mid_part
    grad_branch = grad_middle.astype(BF)
    grad_out = jnp.einsum("td,te->de", attended, grad_branch, preferred_element_type=jnp.float32).astype(BF)
    grad_out_bias = jnp.sum(grad_branch.astype(jnp.float32), axis=0)
    grad_attended = jnp.einsum("te,de->td", grad_branch, out_weight, preferred_element_type=jnp.float32).astype(BF)
    sum_up, sum_down, sum_out = lax.psum((grad_up, grad_down, grad_out), "batch")
    dq, dkn, dkf, dvn, dvf, g = bwd(queries, key_part, partner_k, value_part, partner_v, grad_attended, attended,
                                    e, et, bt, qmisc, kseg, length)
    back_k = from_partner(dkf, "stream", 0)
    back_v = from_partner(dvf, "stream", 0)
    grad_k = (dkn.astype(jnp.float32) + back_k.astype(jnp.float32)).astype(BF)
    grad_v = (dvn.astype(jnp.float32) + back_v.astype(jnp.float32)).astype(BF)
    grad_dist = jnp.einsum("hp,np->nh", g.reshape(heads, 65536).astype(BF), onehot, preferred_element_type=jnp.float32)
    grad_mixed = jnp.concatenate([dq, grad_k, grad_v], axis=1)
    grad_qkv = jnp.einsum("td,te->de", normed, grad_mixed, preferred_element_type=jnp.float32).astype(BF)
    grad_bias_rows = jnp.stack([jnp.sum(dq.astype(jnp.float32), axis=0), jnp.sum(grad_v.astype(jnp.float32), axis=0), grad_out_bias])
    grad_normed = jnp.einsum("te,de->td", grad_mixed, qkv_weight, preferred_element_type=jnp.float32)
    grad_in_part, gain_one, shift_one = norm_back(plain_in, norm_gains[0], norm_shifts[0], grad_normed)
    input_grad = (grad_middle + grad_in_part).astype(BF).reshape(1, rows, length, width)
    small = [jnp.stack([gain_one, gain_two]), jnp.stack([shift_one, shift_two]), grad_bias_rows, grad_dist, grad_up_bias, grad_down_bias]
    flat = jnp.concatenate([s.reshape(-1) for s in small])
    sum_qkv = lax.psum(grad_qkv, "batch")
    flat = lax.psum(flat, "batch")
    parts, at = [], 0
    for s in small:
        parts.append(flat[at:at + s.size].reshape(s.shape)[None])
        at += s.size
    gain, shift, bias, dist, upb, downb = parts
    f32 = lambda a: a.astype(jnp.float32)[None]
    return (output, input_grad, gain, shift, f32(sum_qkv), bias, dist, f32(sum_out), f32(sum_up), upb, f32(sum_down), downb)


def solution(mesh):
    in_specs = (
        P("stream", "batch", None, None),
        P("stream", "batch", None, None),
        P("batch", None),
        P("stream", "batch", None, None),
        P("stream", None, None),
        P("stream", None, None),
        P("stream", None, None),
        P("stream", None, None),
        P("stream", None, None),
        P("stream", None, None),
        P("stream", None, None),
        P("stream", None),
        P("stream", None, None),
        P("stream", None),
    )
    out_specs = (
        P("stream", "batch", None, None),
        P("stream", "batch", None, None),
        P("stream", None, None),
        P("stream", None, None),
        P("stream", None, None),
        P("stream", None, None),
        P("stream", None, None),
        P("stream", None, None),
        P("stream", None, None),
        P("stream", None),
        P("stream", None, None),
        P("stream", None),
    )
    return jax.shard_map(
        on_device, mesh=mesh, in_specs=in_specs, out_specs=out_specs, check_vma=False
    )
```

time: 1410 us -> 637 us (0.45)
  waiting for transfers between devices: 510 us -> 251 us
  matrix products: 363 us -> 121 us
  local copies, waits for them, and re-layouts: 235 us -> 36.4 us
  other arithmetic: 175 us -> 43.4 us
  Pallas kernels: 0 us -> 93.1 us
  loops' own time: 31.4 us -> 0 us
    psum x1, waiting for transfers between devices: 403 us -> 146 us  [on_device(): sum_qkv = lax.psum(grad_qkv, 'batch')]
    dot_general x20 -> x2, matrix products: 247 us -> 6.57 us  [the longest x1 3.59 us: on_device(): jnp.dot(distance_table[0].T.astype(BF), onehot, preferred_element_type=jn...]
    while x117 -> x0, local copies, waits for them, and re-layouts: 128 us -> none
    pallas_call x0 -> x2, Pallas kernels: none -> 93.1 us  [the longest x1 59.5 us: bwd(): pl.pallas_call(functools.partial(bwd_kernel, CK, MODE), grid=(NP, R), in_...]
    add x4 -> x2, other arithmetic: 45.2 us -> 0.89 us  [the longest x1 0.88 us: code_onehot(): step_x * GRID + step_y]
    select_n x4 -> x0, other arithmetic: 43.9 us -> none  [bias_block(): masked_bias = jnp.where(allowed[None], looked, MASKED)]
    dynamic_update_slice x14 -> x0, local copies, waits for them, and re-layouts: 43.5 us -> none  [the longest x10 34.8 us: on_device(): lax.map(backward_row, (by_row(queries), by_row(key_part), by_row(value_pa...]
    convert_element_type x8 -> x10, other arithmetic: 40.4 us -> 6.92 us  [the longest x2 3.52 us: on_device(): normed = layer_norm(plain_in, norm_gains[0], norm_shifts[0]).astype(BF)]
  transfers between devices with their start and end apart: 3 -> 5, of which waited for: 3 -> 5; matrix products, arithmetic and copies ran while one was open for 4% -> 13% of each run, Pallas kernels for 0% -> 0%
where the time goes in v1:
time: 637 us; the launch traced here: 629 us
  waiting for transfers between devices  251 us (39%)
  matrix products  121 us (19%)
  Pallas kernels  93.1 us (15%)
  blocking collectives  64.1 us (10%)
  other arithmetic  43.4 us (7%)
  local copies, waits for them, and re-layouts  36.4 us (6%)
  between operations  15 us (2%)
    psum x1, waiting for transfers between devices, on_device(): sum_qkv = lax.psum(grad_qkv, 'batch')  146 us
    ppermute x4, waiting for transfers between devices, from_partner(): return lax.ppermute(block, axis, route)  105 us
    psum x1, blocking collectives, on_device(): flat = lax.psum(flat, 'batch')  64.1 us
    pallas_call x1, Pallas kernels, bwd(): pl.pallas_call(functools.partial(bwd_kernel, CK, MODE), grid=(NP, R), in_...  59.5 us
    dot_general x1, matrix products, on_device(): jnp.dot(normed_two, up_weight, preferred_element_type=jnp.float32)  35.2 us
    pallas_call x1, Pallas kernels, fwd(): pl.pallas_call(functools.partial(fwd_kernel, CQ), grid=(R, NP), in_specs=...  33.6 us
    dot_general x1, matrix products, on_device(): jnp.einsum('td,fd->tf', cot_bf, down_weight, preferred_element_type=jnp.f...  17.4 us
    broadcast_in_dim x4, other arithmetic, on_device(): f32 = lambda a: a.astype(jnp.float32)[None]  17.1 us
  transfers between devices with their start and end apart: 5, of which 5 were waited for; matrix products, arithmetic and copies ran while one was open for 13% of the time, Pallas kernels for 0%

profile of v1, /device:TPU:0, one launch (start us, length us, event | category | flops | bytes accessed | tf_op | source)
XLA Modules:
  0.0 628.8 jit_solution(9349944437771250888)
XLA Ops:
  7.3 1.8 convert_reduce_fusion.1
  9.1 2.1 fusion.35
  13.2 3.8 fusion.21
  17.0 2.1 fusion.86
  19.1 2.9 collective-permute-start
  22.1 1.4 fusion.23.vn_ref
  23.5 0.9 fusion.62
  25.1 3.6 convolution_convert_fusion
  29.1 1.3 slice.101.b_ref
  32.4 25.2 %collective-permute-done.kf_ref = bf16[1024,768]{1,0:T(8,128)(2,1)} collective-permute-done((bf16[1024,768]{1,0:T(8,128)(2,1)}, bf16[1024,768]{1,0:T(8,128)(2,1)}, u32[]{:S(2)}, u32[]{:S(2)}) %collective-permute-start) | collective-permute-done | bytes 1572896 | tf_op jit(solution)/shard_map/ppermute | solution.py:142
  57.6 32.9 %collective-permute-done.1.vf_ref = bf16[1024,768]{1,0:T(8,128)(2,1)} collective-permute-done((bf16[1024,768]{1,0:T(8,128)(2,1)}, bf16[1024,768]{1,0:T(8,128)(2,1)}, u32[]{:S(2)}, u32[]{:S(2)}) %collective-permute-start.1) | collective-permute-done | bytes 1572896 | tf_op jit(solution)/shard_map/ppermute | solution.py:142
  90.5 33.6 %att_fwd.1 = (bf16[1024,768]{1,0:T(8,128)(2,1)S(1)}, bf16[1024,128]{1,0:T(8,128)(2,1)S(1)}) custom-call(bf16[1024,768]{1,0:T(8,128)(2,1)S(1)} %copy-done.1, bf16[1024,768]{1,0:T(8,128)(2,1)} %get-tuple-element.66.kn_ref, bf16[1024,768]{1,0:T(8,128)(2,1)} %collective-permute-done.kf_ref, bf16[1024,768]{1,0:T(8,128)(2,1)} %fusion.23.vn_ref, ...), custom_call_target="tpu_custom_call" | custom-call | tf_op jit(solution)/shard_map/att_fwd/pallas_call | solution.py:60
  124.1 1.5 fusion.89
  126.2 1.2 slice-done
  127.9 35.2 %multiply_convert_fusion = (bf16[1024,3072]{1,0:T(8,128)(2,1)}, f32[1024,3072]{1,0:T(8,128)}, f32[1024,3072]{1,0:T(8,128)}) fusion(f32[3072]{0:T(1024)S(1)} %bitcast.133, bf16[1,768,3072]{2,1,0:T(8,128)(2,1)S(1)} %bitcast.131, f32[1024,768]{1,0:T(8,128)S(1)} %get-tuple-element.81, f32[768]{0:T(1024)S(1)} %copy-done.28, f32[768]{0:T(1024)S(1)} %get-tuple-element.88, ...), kind=kOutput, calls=%fused_computation.7 | convolution fusion | flops 5043388416 | bytes 39348224 | tf_op jit(solution)/shard_map/dot_general | solution.py:208
  163.1 17.4 %convert_reduce_fusion = (f32[3072]{0:T(1024)}, bf16[1024,3072]{1,0:T(8,128)(2,1)}) fusion(f32[1024,3072]{1,0:T(8,128)} %get-tuple-element.65, bf16[1024,768]{1,0:T(8,128)(2,1)S(1)} %bitcast.111, bf16[1,3072,768]{2,1,0:T(8,128)(2,1)} %param.26, f32[1024,3072]{1,0:T(8,128)} %get-tuple-element.82, f32[3072]{0:T(1024)} %bitcast.132), kind=kOutput, calls=%fused_computation.5 | convolution fusion | flops 4885312512 | bytes 37773312 | tf_op jit(solution)/shard_map/td,fd->tf/dot_general | solution.py:216
  180.5 10.5 %multiply_reduce_fusion = (f32[768]{0:T(1024)}, f32[1024]{0:T(1024)S(1)}, f32[768]{0:T(1024)}, f32[1024,768]{1,0:T(8,128)S(1)}) fusion(f32[1024,768]{1,0:T(8,128)} %copy-done.9, f32[1024]{0:T(1024)S(1)} %fusion.75, f32[1024]{0:T(1024)S(1)} %broadcast_multiply_fusion, f32[768]{0:T(1024)S(1)} %get-tuple-element.88, bf16[1024,3072]{1,0:T(8,128)(2,1)} %get-tuple-element.86, ...), kind=kOutput, calls=%fused_computation.72 | convolution fusion | flops 4838126592 | bytes 17323008 | tf_op jit(solution)/shard_map/tf,df->td/dot_general | solution.py:220
  191.0 1.4 fusion.84
  193.7 2.6 convolution_convert_fusion.4.do_ref
  196.3 2.5 fusion.45
  198.7 59.5 %att_bwd.1 = (bf16[1024,768]{1,0:T(8,128)(2,1)S(1)}, bf16[1024,768]{1,0:T(8,128)(2,1)S(1)}, bf16[1024,768]{1,0:T(8,128)(2,1)}, bf16[1024,768]{1,0:T(8,128)(2,1)}...) custom-call(bf16[1024,768]{1,0:T(8,128)(2,1)} %get-tuple-element.67.q_ref, ...), custom_call_target="tpu_custom_call" | custom-call | tf_op jit(solution)/shard_map/att_bwd/pallas_call | solution.py:128
  258.2 1.8 collective-permute-start.2
  260.3 10.0 %fusion.18 = bf16[1,3072,768]{2,1,0:T(8,128)(2,1)} fusion(bf16[1024,3072]{1,0:T(8,128)(2,1)} %get-tuple-element.64, bf16[1024,768]{1,0:T(8,128)(2,1)S(1)} %bitcast.112), kind=kOutput, calls=%fused_computation.38 | convolution fusion | flops 4834197504 | bytes 12582912 | tf_op jit(solution)/shard_map/tf,td->fd/dot_general | solution.py:214
  270.3 9.9 %fusion.17 = bf16[1,768,3072]{2,1,0:T(8,128)(2,1)} fusion(bf16[1024,3072]{1,0:T(8,128)(2,1)} %get-tuple-element.86, f32[1024,768]{1,0:T(8,128)S(1)} %copy-done.10, f32[768]{0:T(1024)S(1)} %copy-done.28, f32[768]{0:T(1024)S(1)} %get-tuple-element.88, f32[1024]{0:T(1024)S(1)} %fusion.75, f32[1024]{0:T(1024)S(1)} %broadcast_multiply_fusion), kind=kOutput, calls=%fused_computation.37 | convolution fusion | flops 4838129664 | bytes 14170112 | tf_op jit(solution)/shard_map/td,tf->df/dot_general | solution.py:218
  280.2 15.7 %collective-permute-done.2 = bf16[1024,768]{1,0:T(8,128)(2,1)S(1)} collective-permute-done((bf16[1024,768]{1,0:T(8,128)(2,1)}, bf16[1024,768]{1,0:T(8,128)(2,1)S(1)}, u32[]{:S(2)}, u32[]{:S(2)}) %collective-permute-start.2) | collective-permute-done | bytes 1572896 | tf_op jit(solution)/shard_map/ppermute | solution.py:142
  296.3 31.5 %collective-permute-done.3 = bf16[1024,768]{1,0:T(8,128)(2,1)S(1)} collective-permute-done((bf16[1024,768]{1,0:T(8,128)(2,1)}, bf16[1024,768]{1,0:T(8,128)(2,1)S(1)}, u32[]{:S(2)}, u32[]{:S(2)}) %collective-permute-start.3) | collective-permute-done | bytes 1572896 | tf_op jit(solution)/shard_map/ppermute | solution.py:142
  328.4 4.6 fusion.82
  333.0 1.6 fusion.32
  334.6 2.9 fusion.34
  337.5 6.2 fusion.16
  345.0 2.4 convert_reduce_fusion.2
  347.4 1.7 convert_reduce_fusion.5
  349.7 1.3 reshape.295
  351.0 1.3 reshape.292
  352.6 1.2 copy.34
  353.8 3.0 fusion
  356.8 1.4 reshape.298
  358.3 10.0 %add_convert_fusion.4 = bf16[1024,768]{1,0:T(8,128)(2,1)} fusion(f32[1024,768]{1,0:T(8,128)} %copy-done.9, bf16[1024,3072]{1,0:T(8,128)(2,1)} %get-tuple-element.64, bf16[1,3072,768]{2,1,0:T(8,128)(2,1)} %param.26, f32[768]{0:T(1024)S(1)} %copy-done.30), kind=kOutput, calls=%fused_computation.78 | convolution fusion | flops 4834197504 | bytes 15731712 | tf_op jit(solution)/shard_map/dot_general | solution.py:210
  368.9 0.7 reshape.297
  370.3 1.3 pad_maximum_fusion.5
  371.6 1.3 reshape.296
  372.9 1.3 pad_maximum_fusion.4
  374.2 1.3 reshape.293
  375.5 1.3 constant_dynamic-update-slice_fusion.5
  376.8 1.3 constant_dynamic-update-slice_fusion.4
  378.1 1.3 constant_dynamic-update-slice_fusion.3
  379.4 1.3 constant_dynamic-update-slice_fusion.2
  380.8 1.3 constant_dynamic-update-slice_fusion.1
  382.1 1.3 constant_dynamic-update-slice_fusion
  383.3 64.1 %psum.35 = f32[9984]{0:T(1024)} all-reduce(f32[9984]{0:T(1024)} %constant_dynamic-update-slice_fusion), channel_id=1, replica_groups=mesh['stream'=2,'batch'=16] {'batch'}, use_global_device_ids=true, to_apply=%region_17.18 | all-reduce | flops 9984 | bytes 79872 | tf_op jit(solution)/shard_map/psum | solution.py:244
  447.4 0.7 slice.97
  448.2 1.3 slice.99
  449.5 1.3 fusion.87
  450.8 0.7 broadcast_in_dim_reshape.18
  451.5 1.4 copy.27
  452.9 1.4 fusion.88
  454.3 1.3 broadcast_in_dim_reshape.15
  455.6 1.3 broadcast_in_dim_reshape.16
  457.5 1.3 broadcast_in_dim.79
  458.8 145.6 %all-reduce.3.cloned.1.call-done = (bf16[1,768,2304]{2,1,0:T(8,128)(2,1)}, bf16[1,768,768]{2,1,0:T(8,128)(2,1)}, bf16[1,768,3072]{2,1,0:T(8,128)(2,1)}, bf16[1,3072,768]{2,1,0:T(8,128)(2,1)}) async-done(((bf16[1,768,2304]{2,1,0:T(8,128)(2,1)}, bf16[1,768,768]{2,1,0:T(8,128)(2,1)}, bf16[1,768,3072]{2,1,0:T(8,128)(2,1)}, bf16[1,3072,768]{2,1,0:T(8,128)(2,1)}), (bf16[1,768,2304]{2,1,0:T(8,128)(2,1)}, ...) | async-done | bytes 14155792 | tf_op jit(solution)/shard_map/psum | solution.py:243
  604.4 7.5 %broadcast_in_dim.75 = f32[1,768,3072]{2,1,0:T(8,128)} convert(bf16[1,768,3072]{2,1,0:T(8,128)(2,1)} %get-tuple-element.56) | non-fusion elementwise | flops 2359296 | bytes 14155776 | tf_op jit(solution)/shard_map/broadcast_in_dim | solution.py:250
  612.0 4.5 broadcast_in_dim.78
  616.4 3.5 broadcast_in_dim.71
  619.9 1.6 broadcast_in_dim.73
  (118 shorter events, 12.8 us)
Async XLA Ops:
  7.2 6.0 copy-start
  7.2 597.2 %all-reduce.3.cloned.1.call-start = ((), (), s32[]{:S(2)}) async-start(), calls=%async_computation | async-start | bytes 28311552 | tf_op jit(solution)/shard_map/psum | solution.py:243
  7.2 4.0 copy-start.24
  7.2 4.6 copy-start.26
  7.3 4.6 copy-start.27
  7.3 5.2 copy-start.5
  12.5 0.6 copy-start.17
  12.5 0.7 copy-start.19
  19.1 5.3 copy-start.29
  19.1 38.5 %collective-permute-start = (bf16[1024,768]{1,0:T(8,128)(2,1)}, bf16[1024,768]{1,0:T(8,128)(2,1)}, u32[]{:S(2)}, u32[]{:S(2)}) collective-permute-start(bf16[1024,768]{1,0:T(8,128)(2,1)} %get-tuple-element.66.kn_ref), channel_id=1, source_target_pairs={{0,16},{16,0},{1,17},{17,1},{2,18},{18,2},{3,19},{19,3},{4,20},{20... | collective-permute-start | bytes 4718600 | tf_op jit(solution)/shard_map/ppermute | solution.py:142
  23.5 67.0 %collective-permute-start.1 = (bf16[1024,768]{1,0:T(8,128)(2,1)}, bf16[1024,768]{1,0:T(8,128)(2,1)}, u32[]{:S(2)}, u32[]{:S(2)}) collective-permute-start(bf16[1024,768]{1,0:T(8,128)(2,1)} %fusion.23.vn_ref), channel_id=1, source_target_pairs={{0,16},{16,0},{1,17},{17,1},{2,18},{18,2},{3,19},{19,3},{4,20},{20... | collective-permute-start | bytes 4718600 | tf_op jit(solution)/shard_map/ppermute | solution.py:142
  28.6 2.9 copy-start.25
  29.1 61.3 %copy-start.1 = (bf16[1024,768]{1,0:T(8,128)(2,1)S(1)}, bf16[1024,768]{1,0:T(8,128)(2,1)}, u32[]{:S(2)}) copy-start(bf16[1024,768]{1,0:T(8,128)(2,1)} %get-tuple-element.67.q_ref) | copy-start | bytes 4718596
  90.5 33.6 %copy-start.6 = (bf16[1,2,512,768]{3,2,1,0:T(8,128)(2,1)S(1)}, bf16[1,2,512,768]{3,2,1,0:T(8,128)(2,1)}, u32[]{:S(2)}) copy-start(bf16[1,2,512,768]{3,2,1,0:T(8,128)(2,1)} %param.14) | copy-start | bytes 4718596
  90.5 33.6 %copy-start.31 = (f32[768]{0:T(1024)S(1)}, f32[768]{0:T(1024)}, u32[]{:S(2)}) copy-start(f32[768]{0:T(1024)} %get-tuple-element.47) | copy-start | bytes 9220
  90.5 33.6 %copy-start.33 = (bf16[1,768,768]{2,1,0:T(8,128)(2,1)S(1)}, bf16[1,768,768]{2,1,0:T(8,128)(2,1)}, u32[]{:S(2)}) copy-start(bf16[1,768,768]{2,1,0:T(8,128)(2,1)} %param.23) | copy-start | bytes 3538948
  124.1 1.6 copy-start.2
  124.1 3.3 slice-start
  124.1 3.8 slice-start.1
  125.7 37.5 %copy-start.9 = (f32[1024,768]{1,0:T(8,128)}, f32[1024,768]{1,0:T(8,128)S(1)}, u32[]{:S(2)}) copy-start(f32[1024,768]{1,0:T(8,128)S(1)} %get-tuple-element.81) | copy-start | bytes 9437188
  125.7 2.2 copy-start.28
  125.7 2.2 copy-start.35
  127.9 35.2 %copy-start.8 = (bf16[1,2,512,768]{3,2,1,0:T(8,128)(2,1)S(1)}, bf16[1,2,512,768]{3,2,1,0:T(8,128)(2,1)}, u32[]{:S(2)}) copy-start(bf16[1,2,512,768]{3,2,1,0:T(8,128)(2,1)} %param.15) | copy-start | bytes 4718596
  180.5 10.5 %copy-start.10 = (f32[1024,768]{1,0:T(8,128)S(1)}, f32[1024,768]{1,0:T(8,128)}, u32[]{:S(2)}) copy-start(f32[1024,768]{1,0:T(8,128)} %copy-done.9) | copy-start | bytes 9437188
  192.4 1.3 copy-start.34
  193.7 2.6 copy-start.3
  258.2 79.3 %copy-start.4 = (bf16[1024,768]{1,0:T(8,128)(2,1)}, bf16[1024,768]{1,0:T(8,128)(2,1)S(1)}, u32[]{:S(2)}) copy-start(bf16[1024,768]{1,0:T(8,128)(2,1)S(1)} %get-tuple-element.22) | copy-start | bytes 4718596
  258.2 37.6 %collective-permute-start.2 = (bf16[1024,768]{1,0:T(8,128)(2,1)}, bf16[1024,768]{1,0:T(8,128)(2,1)S(1)}, u32[]{:S(2)}, u32[]{:S(2)}) collective-permute-start(bf16[1024,768]{1,0:T(8,128)(2,1)} %get-tuple-element.24), channel_id=1, source_target_pairs={{0,16},{16,0},{1,17},{17,1},{2,18},{18,2},{3,19},{19,3},{4,20},{20... | collective-permute-start | bytes 4718600 | tf_op jit(solution)/shard_map/ppermute | solution.py:142
  260.0 67.8 %collective-permute-start.3 = (bf16[1024,768]{1,0:T(8,128)(2,1)}, bf16[1024,768]{1,0:T(8,128)(2,1)S(1)}, u32[]{:S(2)}, u32[]{:S(2)}) collective-permute-start(bf16[1024,768]{1,0:T(8,128)(2,1)} %get-tuple-element.26), channel_id=1, source_target_pairs={{0,16},{16,0},{1,17},{17,1},{2,18},{18,2},{3,19},{19,3},{4,20},{20... | collective-permute-start | bytes 4718600 | tf_op jit(solution)/shard_map/ppermute | solution.py:142
  280.2 47.6 %copy-start.14 = (bf16[1024,768]{1,0:T(8,128)(2,1)S(1)}, bf16[1024,768]{1,0:T(8,128)(2,1)}, u32[]{:S(2)}) copy-start(bf16[1024,768]{1,0:T(8,128)(2,1)} %get-tuple-element.25) | copy-start | bytes 4718596
  296.2 32.1 %copy-start.7 = (bf16[1,2,512,768]{3,2,1,0:T(8,128)(2,1)S(1)}, bf16[1,2,512,768]{3,2,1,0:T(8,128)(2,1)}, u32[]{:S(2)}) copy-start(bf16[1,2,512,768]{3,2,1,0:T(8,128)(2,1)} %param.14) | copy-start | bytes 4718596
  296.3 32.1 %copy-start.18 = (f32[768]{0:T(1024)S(1)}, f32[768]{0:T(1024)}, u32[]{:S(2)}) copy-start(f32[768]{0:T(1024)} %copy-done.17) | copy-start | bytes 9220
  296.3 32.1 %copy-start.21 = (f32[1,4,2,128]{3,1,2,0:T(4,128)S(1)}, f32[1,4,2,128]{3,1,2,0:T(4,128)}, u32[]{:S(2)}) copy-start(f32[1,4,2,128]{3,1,2,0:T(4,128)} %copy.33) | copy-start | bytes 12292
  328.4 4.6 copy-start.22
  333.0 1.6 copy-start.20
  343.7 0.7 copy-start.32
  345.0 7.2 %copy-start.13 = (f32[12,256,256]{2,1,0:T(8,128)S(1)}, f32[12,256,256]{2,1,0:T(8,128)}, u32[]{:S(2)}) copy-start(f32[12,256,256]{2,1,0:T(8,128)} %get-tuple-element.27) | copy-start | bytes 9437188
  352.4 1.4 copy-start.16
  353.8 4.4 copy-start.30
  358.2 10.0 %copy-start.23 = (f32[1,768]{1,0:T(1,128)S(1)}, f32[1,768]{1,0:T(1,128)}, u32[]{:S(2)}) copy-start(f32[1,768]{1,0:T(1,128)} %stack.24) | copy-start | bytes 9220
  604.4 7.5 %copy-start.11 = (bf16[1,3072,768]{2,1,0:T(8,128)(2,1)S(1)}, bf16[1,3072,768]{2,1,0:T(8,128)(2,1)}, u32[]{:S(2)}) copy-start(bf16[1,3072,768]{2,1,0:T(8,128)(2,1)} %get-tuple-element.57) | copy-start | bytes 14155780
  612.0 4.5 copy-start.12
  616.4 3.5 copy-start.15
Sparse Core Ops, SparseCore 0:
  343.8 260.5 all-reduce.2

commit v2 on v1

--- a/solution.py
+++ b/solution.py
@@ -132,6 +132,161 @@
         compiler_params=pltpu.CompilerParams(vmem_limit_bytes=48<<20),name="att_bwd")(q,kn,kf,vn,vf,do,o,e,et,bt,qmisc,kseg)
 
 
+F32=jnp.float32
+SIDE=768
+WIDE=384
+LAG=3
+
+def bit_orders(n, count):
+    bits=n.bit_length()-1
+    plain=list(range(bits))
+    other=[0]+plain[2:]+[1] if bits>2 else plain
+    return [other if c%5==3 else plain for c in range(count)]
+
+def plan_of(n, order, rows):
+    sizes=[rows]
+    for _ in order:
+        m=sizes[-1]
+        sizes.append(m//2 if m%32==0 else m)
+    return sizes
+
+def place(me, b):
+    bit=(me//(1<<b))%2
+    return bit, me+(1-2*bit)*(1<<b)
+
+class Engine:
+    def __init__(self, n, orders, x, y, recv, offs, send_sem, recv_sem, me):
+        self.n,self.orders,self.x,self.y,self.recv,self.offs=n,orders,x,y,recv,offs
+        self.ss,self.rs,self.me=send_sem,recv_sem,me
+        self.bits=n.bit_length()-1
+        self.pending={}
+    def seg(self,c,upto):
+        sizes=plan_of(self.n,self.orders[c],SIDE); off=0
+        for s in range(upto):
+            if sizes[s+1]!=sizes[s]:
+                off=off+place(self.me,self.orders[c][s])[0]*sizes[s+1]
+        return off,sizes[upto]
+    def ds(self,off,size):
+        return pl.ds(off if isinstance(off,int) else pl.multiple_of(off,16),size)
+    def start(self,c,stage):
+        B=self.bits; order=self.orders[c]; sizes=plan_of(self.n,order,SIDE)
+        if stage<B:
+            b=order[stage]; bit,partner=place(self.me,b)
+            off,m=self.seg(c,stage)
+            if sizes[stage+1]!=m:
+                src=self.x.at[c,self.ds(off+(1-bit)*(m//2),m//2)]
+            else:
+                src=self.x.at[c,self.ds(off,m)]
+            dst=self.recv.at[c,pl.ds(self.offs[c][stage],sizes[stage+1])]
+        else:
+            s=2*B-1-stage
+            if sizes[s+1]==sizes[s]: return
+            b=order[s]; bit,partner=place(self.me,b)
+            off,m=self.seg(c,s+1)
+            src=self.y.at[c,self.ds(off,m)]; dst=src
+        d=pltpu.make_async_remote_copy(src,dst,self.ss.at[c,stage],self.rs.at[c,stage],
+            device_id={"batch":partner},device_id_type=pl.DeviceIdType.MESH)
+        d.start(); self.pending[(c,stage)]=d
+    def finish(self,c,stage):
+        B=self.bits; order=self.orders[c]; sizes=plan_of(self.n,order,SIDE)
+        d=self.pending.pop((c,stage),None)
+        if d is None: return
+        d.wait()
+        if stage<B:
+            off,m=self.seg(c,stage+1); ro=self.offs[c][stage]; x,recv=self.x,self.recv
+            to=self.y if stage==B-1 else x
+            step=48
+            def body(i,_):
+                at=self.ds(off+i*step,step)
+                to[c,at]=(x[c,at].astype(F32)+recv[c,pl.ds(pl.multiple_of(ro+i*step,16),step)].astype(F32)).astype(BF)
+                return 0
+            lax.fori_loop(0,m//step,body,0)
+
+def recv_offsets(n, orders):
+    res=[]
+    for o in orders:
+        sizes=plan_of(n,o,SIDE); at=[0]
+        for s in range(len(o)): at.append(at[-1]+sizes[s+1])
+        res.append(at)
+    return res
+
+def barrier(n, me):
+    sem=pltpu.get_barrier_semaphore()
+    bits=n.bit_length()-1
+    for b in range(bits):
+        pl.semaphore_signal(sem,inc=1,device_id={"batch":place(me,b)[1]},device_id_type=pl.DeviceIdType.MESH)
+    pl.semaphore_wait(sem,bits)
+
+def ar_kernel(n, layout, with_small, *refs):
+    na=max(a for a,_,_ in layout)+1
+    ins=refs[:na]; refs=refs[na:]
+    if with_small: small_in,refs=refs[0],refs[1:]
+    outs=refs[:na]; refs=refs[na:]
+    if with_small: small_out,refs=refs[0],refs[1:]
+    x,y,recv,in_sem,out_sem,ss,rs=refs[:7]
+    C=len(layout)
+    me=lax.axis_index("batch")
+    orders=bit_orders(n,C); offs=recv_offsets(n,orders)
+    def view(ref,a,r,c): return ref.at[pl.ds(r*SIDE,SIDE),pl.ds(c*WIDE,WIDE)]
+    loads=[]
+    for c,(a,r,k) in enumerate(layout):
+        d=pltpu.make_async_copy(view(ins[a],a,r,k),x.at[c],in_sem.at[c]); d.start(); loads.append(d)
+    barrier(n,me)
+    eng=Engine(n,orders,x,y,recv,offs,ss,rs,me)
+    B=eng.bits
+    if with_small:
+        small_x,small_recv,small_sem,small_ss,small_rs=refs[7:12]
+        d=pltpu.make_async_copy(small_in,small_x.at[0],small_sem); d.start(); d.wait()
+    def small_copy(s):
+        return pltpu.make_async_remote_copy(small_x.at[s],small_recv.at[s],small_ss.at[s],small_rs.at[s],
+            device_id={"batch":place(me,s)[1]},device_id_type=pl.DeviceIdType.MESH)
+    small_d=None
+    stores={}
+    for t in range(C+LAG*2*B):
+        if with_small and t%LAG==0 and t//LAG<=B:
+            i=t//LAG
+            if i>0:
+                small_d.wait()
+                small_x[i]=small_x[i-1]+small_recv[i-1]
+            if i<B:
+                small_d=small_copy(i); small_d.start()
+            else:
+                small_d=pltpu.make_async_copy(small_x.at[i],small_out,small_sem); small_d.start()
+        for s in range(2*B,-1,-1):
+            c=t-LAG*s
+            if not 0<=c<C: continue
+            if s==0: loads[c].wait()
+            else: eng.finish(c,s-1)
+            if s<2*B: eng.start(c,s)
+            else:
+                a,r,k=layout[c]
+                d=pltpu.make_async_copy(y.at[c],view(outs[a],a,r,k),out_sem.at[c]); d.start(); stores[c]=d
+    for c in range(C): stores[c].wait()
+    if with_small: small_d.wait()
+
+def allreduce(arrays, n, collective_id, small=None):
+    layout=[]
+    for a,arr in enumerate(arrays):
+        for r in range(arr.shape[0]//SIDE):
+            for k in range(arr.shape[1]//WIDE): layout.append((a,r,k))
+    C=len(layout); bits=n.bit_length()-1
+    rows=max(o[-1] for o in recv_offsets(n,bit_orders(n,C)))
+    scratch=[pltpu.VMEM((C,SIDE,WIDE),BF),pltpu.VMEM((C,SIDE,WIDE),BF),pltpu.VMEM((C,rows,WIDE),BF),
+            pltpu.SemaphoreType.DMA((C,)),pltpu.SemaphoreType.DMA((C,)),pltpu.SemaphoreType.DMA((C,2*bits)),pltpu.SemaphoreType.DMA((C,2*bits))]
+    extra=[]
+    if small is not None:
+        extra=[small]
+        scratch+=[pltpu.VMEM((bits+1,)+small.shape,F32),pltpu.VMEM((bits,)+small.shape,F32),pltpu.SemaphoreType.DMA,
+            pltpu.SemaphoreType.DMA((bits,)),pltpu.SemaphoreType.DMA((bits,))]
+    return pl.pallas_call(functools.partial(ar_kernel,n,layout,small is not None),
+        in_specs=[pl.BlockSpec(memory_space=pl.ANY)]*(len(arrays)+len(extra)),
+        out_specs=[pl.BlockSpec(memory_space=pl.ANY)]*(len(arrays)+len(extra)),
+        out_shape=[jax.ShapeDtypeStruct(a.shape,a.dtype) for a in list(arrays)+extra],
+        scratch_shapes=scratch,
+        compiler_params=pltpu.CompilerParams(collective_id=collective_id,has_side_effects=True,vmem_limit_bytes=60<<20),
+        name="weight_sum")(*arrays,*extra)
+
+
 def from_partner(block, axis, stride):
     count = lax.axis_size(axis)
     route = []
@@ -224,7 +379,6 @@
     grad_out = jnp.einsum("td,te->de", attended, grad_branch, preferred_element_type=jnp.float32).astype(BF)
     grad_out_bias = jnp.sum(grad_branch.astype(jnp.float32), axis=0)
     grad_attended = jnp.einsum("te,de->td", grad_branch, out_weight, preferred_element_type=jnp.float32).astype(BF)
-    sum_up, sum_down, sum_out = lax.psum((grad_up, grad_down, grad_out), "batch")
     dq, dkn, dkf, dvn, dvf, g = bwd(queries, key_part, partner_k, value_part, partner_v, grad_attended, attended,
                                     e, et, bt, qmisc, kseg, length)
     back_k = from_partner(dkf, "stream", 0)
@@ -240,8 +394,11 @@
     input_grad = (grad_middle + grad_in_part).astype(BF).reshape(1, rows, length, width)
     small = [jnp.stack([gain_one, gain_two]), jnp.stack([shift_one, shift_two]), grad_bias_rows, grad_dist, grad_up_bias, grad_down_bias]
     flat = jnp.concatenate([s.reshape(-1) for s in small])
-    sum_qkv = lax.psum(grad_qkv, "batch")
-    flat = lax.psum(flat, "batch")
+    rows_of = -(-flat.size // 1024) * 8
+    flat = jnp.pad(flat, (0, rows_of * 128 - flat.size)).reshape(rows_of, 128)
+    sum_up, sum_down, sum_out, sum_qkv, flat = allreduce(
+        [grad_up, grad_down, grad_out, grad_qkv], lax.axis_size("batch"), 3, flat)
+    flat = flat.reshape(-1)
     parts, at = [], 0
     for s in small:
         parts.append(flat[at:at + s.size].reshape(s.shape)[None])

time: 637 us -> 573 us (0.90)
  Pallas kernels: 93.1 us -> 256 us
  waiting for transfers between devices: 251 us -> 89.5 us
  blocking collectives: 64.1 us -> 0 us
  between operations: 15 us -> 1.66 us
  other arithmetic: 43.4 us -> 56 us
    pallas_call x0 -> x1, Pallas kernels: none -> 164 us  [allreduce(): pl.pallas_call(functools.partial(ar_kernel, n, layout, small is not None)...]
    psum x1 -> x0, waiting for transfers between devices: 146 us -> none  [on_device(): sum_qkv = lax.psum(grad_qkv, 'batch')]
    psum x1 -> x0, blocking collectives: 64.1 us -> none  [on_device(): flat = lax.psum(flat, 'batch')]
    ppermute x4, waiting for transfers between devices: 105 us -> 89.5 us  [from_partner(): return lax.ppermute(block, axis, route)]
    unnamed x88 -> x102, local copies, waits for them, and re-layouts: 14.2 us -> 17.6 us
  transfers between devices with their start and end apart: 5 -> 4, of which waited for: 5 -> 4; matrix products, arithmetic and copies ran while one was open for 13% -> 8% of each run, Pallas kernels for 0% -> 0%
where the time goes in v2:
time: 573 us; the launch traced here: 565 us
  Pallas kernels  256 us (45%)
  matrix products  119 us (21%)
  waiting for transfers between devices  89.5 us (16%)
  other arithmetic  56 us (10%)
  local copies, waits for them, and re-layouts  36.7 us (6%)
    pallas_call x1, Pallas kernels, allreduce(): pl.pallas_call(functools.partial(ar_kernel, n, layout, small is not None)...  164 us
    ppermute x4, waiting for transfers between devices, from_partner(): return lax.ppermute(block, axis, route)  89.5 us
    pallas_call x1, Pallas kernels, bwd(): pl.pallas_call(functools.partial(bwd_kernel, CK, MODE), grid=(NP, R), in_...  59.6 us
    dot_general x1, matrix products, on_device(): jnp.dot(normed_two, up_weight, preferred_element_type=jnp.float32)  35.2 us
    pallas_call x1, Pallas kernels, fwd(): pl.pallas_call(functools.partial(fwd_kernel, CQ), grid=(R, NP), in_specs=...  33.2 us
    unnamed x102, local copies, waits for them, and re-layouts  17.6 us
    dot_general x1, matrix products, on_device(): jnp.einsum('td,fd->tf', cot_bf, down_weight, preferred_element_type=jnp.f...  17.3 us
    broadcast_in_dim x4, other arithmetic, on_device(): f32 = lambda a: a.astype(jnp.float32)[None]  17.1 us
  transfers between devices with their start and end apart: 4, of which 4 were waited for; matrix products, arithmetic and copies ran while one was open for 8% of the time, Pallas kernels for 0%

profile of v2, /device:TPU:0, one launch (start us, length us, event | category | flops | bytes accessed | tf_op | source)
XLA Modules:
  0.0 564.6 jit_solution(6052571113816699129)
XLA Ops:
  0.7 1.8 convert_reduce_fusion.1
  2.6 2.2 fusion.32
  6.6 3.8 fusion.18
  10.5 2.1 fusion.82
  12.6 2.9 collective-permute-start
  15.5 1.4 fusion.20.vn_ref
  16.9 0.9 fusion.58
  19.2 3.6 convolution_convert_fusion
  23.3 1.3 slice.93.b_ref
  25.7 1.3 reduce.10
  27.0 2.4 convert_reduce_fusion.2
  29.4 0.8 slice_add_fusion.2
  31.0 20.1 %collective-permute-done.kf_ref = bf16[1024,768]{1,0:T(8,128)(2,1)} collective-permute-done((bf16[1024,768]{1,0:T(8,128)(2,1)}, bf16[1024,768]{1,0:T(8,128)(2,1)}, u32[]{:S(2)}, u32[]{:S(2)}) %collective-permute-start) | collective-permute-done | bytes 1572896 | tf_op jit(solution)/shard_map/ppermute | solution.py:297
  51.1 32.9 %collective-permute-done.1.vf_ref = bf16[1024,768]{1,0:T(8,128)(2,1)} collective-permute-done((bf16[1024,768]{1,0:T(8,128)(2,1)}, bf16[1024,768]{1,0:T(8,128)(2,1)}, u32[]{:S(2)}, u32[]{:S(2)}) %collective-permute-start.1) | collective-permute-done | bytes 1572896 | tf_op jit(solution)/shard_map/ppermute | solution.py:297
  83.9 33.2 %att_fwd.1 = (bf16[1024,768]{1,0:T(8,128)(2,1)S(1)}, bf16[1024,128]{1,0:T(8,128)(2,1)S(1)}) custom-call(bf16[1024,768]{1,0:T(8,128)(2,1)S(1)} %copy-done.1, bf16[1024,768]{1,0:T(8,128)(2,1)} %get-tuple-element.84.kn_ref, bf16[1024,768]{1,0:T(8,128)(2,1)} %collective-permute-done.kf_ref, bf16[1024,768]{1,0:T(8,128)(2,1)} %fusion.20.vn_ref, ...), custom_call_target="tpu_custom_call" | custom-call | tf_op jit(solution)/shard_map/att_fwd/pallas_call | solution.py:60
  117.2 1.5 fusion.84
  119.3 1.1 slice-done
  121.0 35.2 %multiply_convert_fusion = (bf16[1024,3072]{1,0:T(8,128)(2,1)}, f32[1024,3072]{1,0:T(8,128)}, f32[1024,3072]{1,0:T(8,128)}) fusion(f32[3072]{0:T(1024)S(1)} %bitcast.145, bf16[1,768,3072]{2,1,0:T(8,128)(2,1)S(1)} %bitcast.144, f32[1024,768]{1,0:T(8,128)S(1)} %get-tuple-element.98, f32[768]{0:T(1024)S(1)} %copy-done.33, f32[768]{0:T(1024)S(1)} %get-tuple-element.105, ...), kind=kOutput, calls=%fused_computation.7 | convolution fusion | flops 5043388416 | bytes 39348224 | tf_op jit(solution)/shard_map/dot_general | solution.py:363
  156.2 17.3 %convert_reduce_fusion = (f32[3072]{0:T(1024)}, bf16[1024,3072]{1,0:T(8,128)(2,1)}) fusion(f32[1024,3072]{1,0:T(8,128)} %get-tuple-element.83, bf16[1024,768]{1,0:T(8,128)(2,1)S(1)} %bitcast.123, bf16[1,3072,768]{2,1,0:T(8,128)(2,1)} %param.26, f32[1024,3072]{1,0:T(8,128)} %get-tuple-element.99, f32[3072]{0:T(1024)S(1)} %bitcast.146), kind=kOutput, calls=%fused_computation.5 | convolution fusion | flops 4885312512 | bytes 37773312 | tf_op jit(solution)/shard_map/td,fd->tf/dot_general | solution.py:371
  173.5 10.3 %multiply_reduce_fusion = (f32[768]{0:T(1024)S(1)}, f32[1024]{0:T(1024)S(1)}, f32[768]{0:T(1024)S(1)}, f32[1024,768]{1,0:T(8,128)S(1)}) fusion(f32[1024,768]{1,0:T(8,128)} %copy-done.12, f32[1024]{0:T(1024)S(1)} %fusion.71, f32[1024]{0:T(1024)S(1)} %broadcast_multiply_fusion, f32[768]{0:T(1024)S(1)} %get-tuple-element.105, ...), kind=kOutput, calls=%fused_computation.72 | convolution fusion | flops 4838126592 | bytes 17323008 | tf_op jit(solution)/shard_map/tf,df->td/dot_general | solution.py:375
  183.8 7.9 %convolution_convert_fusion.2.refs_0_ = bf16[768,3072]{1,0:T(8,128)(2,1)} fusion(bf16[1024,3072]{1,0:T(8,128)(2,1)S(1)} %copy-done.39, f32[1024,768]{1,0:T(8,128)S(1)} %copy-done.13, f32[768]{0:T(1024)S(1)} %copy-done.33, f32[768]{0:T(1024)S(1)} %get-tuple-element.105, f32[1024]{0:T(1024)S(1)} %fusion.71, f32[1024]{0:T(1024)S(1)} %broadcast_multiply_fusion), kind=kOutput, calls=%fused_computation.24 | convolution fusion | flops 4838129664 | bytes 14170112 | tf_op jit(solution)/shard_map/td,tf->df/dot_general | solution.py:373
  191.7 1.4 fusion.80
  193.8 1.0 copy-done.10
  195.4 2.6 convolution_convert_fusion.4.do_ref
  198.0 2.5 convolution_convert_fusion.5.refs_2_
  200.5 59.6 %att_bwd.1 = (bf16[1024,768]{1,0:T(8,128)(2,1)S(1)}, bf16[1024,768]{1,0:T(8,128)(2,1)S(1)}, bf16[1024,768]{1,0:T(8,128)(2,1)}, bf16[1024,768]{1,0:T(8,128)(2,1)}...) custom-call(bf16[1024,768]{1,0:T(8,128)(2,1)} %get-tuple-element.85.q_ref, ...), custom_call_target="tpu_custom_call" | custom-call | tf_op jit(solution)/shard_map/att_bwd/pallas_call | solution.py:128
  260.1 1.8 collective-permute-start.3
  262.1 2.1 convert_element_type.170
  264.4 1.2 copy.37
  265.6 3.0 fusion
  268.6 7.0 %convolution_convert_fusion.1.refs_1_ = bf16[3072,768]{1,0:T(8,128)(2,1)} fusion(bf16[1024,3072]{1,0:T(8,128)(2,1)S(1)} %bitcast.149, bf16[1024,768]{1,0:T(8,128)(2,1)S(1)} %bitcast.124), kind=kOutput, calls=%fused_computation.23 | convolution fusion | flops 4834197504 | bytes 12582912 | tf_op jit(solution)/shard_map/tf,td->fd/dot_general | solution.py:369
  277.1 1.4 reshape.306
  278.6 10.2 %add_convert_fusion.4 = bf16[1024,768]{1,0:T(8,128)(2,1)} fusion(f32[1024,768]{1,0:T(8,128)} %copy-done.12, bf16[1024,3072]{1,0:T(8,128)(2,1)} %get-tuple-element.82, bf16[1,3072,768]{2,1,0:T(8,128)(2,1)} %param.26, f32[768]{0:T(1024)S(1)} %copy-done.34), kind=kOutput, calls=%fused_computation.78 | convolution fusion | flops 4834197504 | bytes 15731712 | tf_op jit(solution)/shard_map/dot_general | solution.py:365
  288.8 9.0 %collective-permute-done.3 = bf16[1024,768]{1,0:T(8,128)(2,1)} collective-permute-done((bf16[1024,768]{1,0:T(8,128)(2,1)}, bf16[1024,768]{1,0:T(8,128)(2,1)}, u32[]{:S(2)}, u32[]{:S(2)}) %collective-permute-start.3) | collective-permute-done | bytes 1572896 | tf_op jit(solution)/shard_map/ppermute | solution.py:297
  297.8 3.1 convert_reduce_fusion.4
  301.5 0.7 reshape.305
  302.2 27.5 %collective-permute-done.2 = bf16[1024,768]{1,0:T(8,128)(2,1)} collective-permute-done((bf16[1024,768]{1,0:T(8,128)(2,1)}, bf16[1024,768]{1,0:T(8,128)(2,1)}, u32[]{:S(2)}, u32[]{:S(2)}) %collective-permute-start.2) | collective-permute-done | bytes 1572896 | tf_op jit(solution)/shard_map/ppermute | solution.py:297
  329.8 2.3 add_convert_fusion.3
  332.1 6.0 %fusion.78 = (f32[768]{0:T(1024)S(1)}, f32[1024]{0:T(1024)}, f32[1024,768]{1,0:T(8,128)}) fusion(f32[768]{0:T(1024)S(1)} %copy-done.22, f32[1024]{0:T(1024)S(1)} %bitcast.137, bf16[1,2,512,768]{3,2,1,0:T(8,128)(2,1)S(1)} %copy-done.9, bf16[1,768,2304]{2,1,0:T(8,128)(2,1)S(1)} %copy-done, bf16[1024,768]{1,0:T(8,128)(2,1)S(1)} %copy-done.16, ...), kind=kOutput, calls=%fused_computation.174 | convolution fusion | flops 3642751232 | bytes 12990464 | tf_op jit(solution)/shard_map/te,de->td/dot_general | solution.py:392
  338.7 1.3 reshape.304
  340.7 5.2 fusion.31
  346.5 1.3 reshape.301
  347.8 1.3 constant_dynamic-update-slice_fusion.5
  349.1 1.3 constant_dynamic-update-slice_fusion.4
  350.5 1.3 constant_dynamic-update-slice_fusion.3
  351.8 1.3 constant_dynamic-update-slice_fusion.2
  353.1 1.3 constant_dynamic-update-slice_fusion.1
  354.4 1.3 constant_dynamic-update-slice_fusion
  355.6 1.4 pad_bitcast_fusion.refs_4_
  357.0 8.5 %convolution_convert_fusion.3.refs_3_ = bf16[768,2304]{1,0:T(8,128)(2,1)} fusion(bf16[1024,768]{1,0:T(8,128)(2,1)} %get-tuple-element.86, bf16[1024,768]{1,0:T(8,128)(2,1)} %get-tuple-element.77, bf16[1024,768]{1,0:T(8,128)(2,1)} %copy-done.18, bf16[1024,768]{1,0:T(8,128)(2,1)} %copy-done.4), kind=kOutput, calls=%fused_computation.25 | convolution fusion | flops 3639803904 | bytes 9830400 | tf_op jit(solution)/shard_map/td,te->de/dot_general | solution.py:390
  365.5 163.5 %weight_sum.1 = (bf16[768,3072]{1,0:T(8,128)(2,1)}, bf16[3072,768]{1,0:T(8,128)(2,1)}, bf16[768,768]{1,0:T(8,128)(2,1)}, bf16[768,2304]{1,0:T(8,128)(2,1)}, f32[80,128]{1,0:T(8,128)}) custom-call(bf16[768,3072]{1,0:T(8,128)(2,1)} %convolution_convert_fusion.2.refs_0_, bf16[3072,768]{1,0:T(8,128)(2,1)} %convolution_convert_fusion.1.refs_1_, ...), custom_call_target="tpu_custom_call" | custom-call | tf_op jit(solution)/shard_map/weight_sum/pallas_call | solution.py:281
  529.1 1.3 slice_bitcast_fusion
  530.4 1.4 fusion.83
  532.5 1.3 slice.86
  533.8 7.0 %bitcast_convert_fusion = f32[1,3072,768]{2,1,0:T(8,128)} fusion(bf16[3072,768]{1,0:T(8,128)(2,1)} %get-tuple-element.37), kind=kLoop, calls=%fused_computation.29 | loop fusion | flops 2359296 | bytes 14155776 | tf_op jit(solution)/shard_map/broadcast_in_dim | solution.py:407
  540.7 5.0 bitcast_convert_fusion.1
  545.8 3.5 bitcast_convert_fusion.2
  549.3 1.6 bitcast_convert_fusion.3
  550.8 1.4 broadcast_in_dim_reshape.18
  552.2 1.4 copy.30
  553.7 1.3 broadcast_in_dim_reshape.15
  555.0 1.3 broadcast_in_dim_reshape.16
  556.9 1.3 copy.44
  558.8 5.4 add_convert_fusion.1
  (129 shorter events, 14.4 us)
Async XLA Ops:
  0.6 6.0 %copy-start = (bf16[1,768,2304]{2,1,0:T(8,128)(2,1)S(1)}, bf16[1,768,2304]{2,1,0:T(8,128)(2,1)}, u32[]{:S(2)}) copy-start(bf16[1,768,2304]{2,1,0:T(8,128)(2,1)} %param.20) | copy-start | bytes 10616836
  0.7 5.3 copy-start.7
  0.7 4.1 copy-start.30
  0.7 4.7 copy-start.32
  0.7 4.7 copy-start.31
  6.0 0.6 copy-start.21
  6.0 0.7 copy-start.24
  12.6 38.5 %collective-permute-start = (bf16[1024,768]{1,0:T(8,128)(2,1)}, bf16[1024,768]{1,0:T(8,128)(2,1)}, u32[]{:S(2)}, u32[]{:S(2)}) collective-permute-start(bf16[1024,768]{1,0:T(8,128)(2,1)} %get-tuple-element.84.kn_ref), channel_id=1, source_target_pairs={{0,16},{16,0},{1,17},{17,1},{2,18},{18,2},{3,19},{19,3},{4,20},{20... | collective-permute-start | bytes 4718600 | tf_op jit(solution)/shard_map/ppermute | solution.py:297
  16.9 67.0 %collective-permute-start.1 = (bf16[1024,768]{1,0:T(8,128)(2,1)}, bf16[1024,768]{1,0:T(8,128)(2,1)}, u32[]{:S(2)}, u32[]{:S(2)}) collective-permute-start(bf16[1024,768]{1,0:T(8,128)(2,1)} %fusion.20.vn_ref), channel_id=1, source_target_pairs={{0,16},{16,0},{1,17},{17,1},{2,18},{18,2},{3,19},{19,3},{4,20},{20... | collective-permute-start | bytes 4718600 | tf_op jit(solution)/shard_map/ppermute | solution.py:297
  27.0 56.9 %copy-start.1 = (bf16[1024,768]{1,0:T(8,128)(2,1)S(1)}, bf16[1024,768]{1,0:T(8,128)(2,1)}, u32[]{:S(2)}) copy-start(bf16[1024,768]{1,0:T(8,128)(2,1)} %get-tuple-element.85.q_ref) | copy-start | bytes 4718596
  83.9 33.2 %copy-start.8 = (bf16[1,2,512,768]{3,2,1,0:T(8,128)(2,1)S(1)}, bf16[1,2,512,768]{3,2,1,0:T(8,128)(2,1)}, u32[]{:S(2)}) copy-start(bf16[1,2,512,768]{3,2,1,0:T(8,128)(2,1)} %param.14) | copy-start | bytes 4718596
  83.9 33.2 %copy-start.35 = (f32[768]{0:T(1024)S(1)}, f32[768]{0:T(1024)}, u32[]{:S(2)}) copy-start(f32[768]{0:T(1024)} %get-tuple-element.69) | copy-start | bytes 9220
  83.9 33.2 %copy-start.36 = (bf16[1,768,768]{2,1,0:T(8,128)(2,1)S(1)}, bf16[1,768,768]{2,1,0:T(8,128)(2,1)}, u32[]{:S(2)}) copy-start(bf16[1,768,768]{2,1,0:T(8,128)(2,1)} %param.23) | copy-start | bytes 3538948
  117.1 1.6 copy-start.2
  117.2 3.3 slice-start
  117.2 3.8 slice-start.1
  118.8 37.4 %copy-start.12 = (f32[1024,768]{1,0:T(8,128)}, f32[1024,768]{1,0:T(8,128)S(1)}, u32[]{:S(2)}) copy-start(f32[1024,768]{1,0:T(8,128)S(1)} %get-tuple-element.98) | copy-start | bytes 9437188
  118.8 2.2 copy-start.33
  118.8 2.2 copy-start.38
  121.0 35.2 %copy-start.11 = (bf16[1,2,512,768]{3,2,1,0:T(8,128)(2,1)S(1)}, bf16[1,2,512,768]{3,2,1,0:T(8,128)(2,1)}, u32[]{:S(2)}) copy-start(bf16[1,2,512,768]{3,2,1,0:T(8,128)(2,1)} %param.15) | copy-start | bytes 4718596
  173.5 10.3 %copy-start.13 = (f32[1024,768]{1,0:T(8,128)S(1)}, f32[1024,768]{1,0:T(8,128)}, u32[]{:S(2)}) copy-start(f32[1024,768]{1,0:T(8,128)} %copy-done.12) | copy-start | bytes 9437188
  173.5 10.3 %copy-start.39 = (bf16[1024,3072]{1,0:T(8,128)(2,1)S(1)}, bf16[1024,3072]{1,0:T(8,128)(2,1)}, u32[]{:S(2)}) copy-start(bf16[1024,3072]{1,0:T(8,128)(2,1)} %get-tuple-element.103) | copy-start | bytes 18874372
  193.2 1.6 copy-start.10
  193.2 1.6 copy-start.23
  193.2 2.2 copy-start.37
  195.4 2.6 copy-start.3
  260.0 4.4 copy-start.6
  260.0 15.6 %copy-start.4 = (bf16[1024,768]{1,0:T(8,128)(2,1)}, bf16[1024,768]{1,0:T(8,128)(2,1)S(1)}, u32[]{:S(2)}) copy-start(bf16[1024,768]{1,0:T(8,128)(2,1)S(1)} %get-tuple-element.27) | copy-start | bytes 4718596
  260.1 37.7 %collective-permute-start.3 = (bf16[1024,768]{1,0:T(8,128)(2,1)}, bf16[1024,768]{1,0:T(8,128)(2,1)}, u32[]{:S(2)}, u32[]{:S(2)}) collective-permute-start(bf16[1024,768]{1,0:T(8,128)(2,1)} %get-tuple-element.31), channel_id=1, source_target_pairs={{0,16},{16,0},{1,17},{17,1},{2,18},{18,2},{3,19},{19,3},{4,20},{20... | collective-permute-start | bytes 4718600 | tf_op jit(solution)/shard_map/ppermute | solution.py:297
  261.9 67.9 %collective-permute-start.2 = (bf16[1024,768]{1,0:T(8,128)(2,1)}, bf16[1024,768]{1,0:T(8,128)(2,1)}, u32[]{:S(2)}, u32[]{:S(2)}) collective-permute-start(bf16[1024,768]{1,0:T(8,128)(2,1)} %get-tuple-element.29), channel_id=1, source_target_pairs={{0,16},{16,0},{1,17},{17,1},{2,18},{18,2},{3,19},{19,3},{4,20},{20... | collective-permute-start | bytes 4718600 | tf_op jit(solution)/shard_map/ppermute | solution.py:297
  264.2 1.4 copy-start.20
  264.4 4.2 slice-start.2
  265.6 3.0 slice-start.3
  268.6 10.0 %copy-start.34 = (f32[768]{0:T(1024)S(1)}, f32[768]{0:T(1024)}, u32[]{:S(2)}) copy-start(f32[768]{0:T(1024)} %reduce.10) | copy-start | bytes 9220
  278.6 19.2 %copy-start.17 = (bf16[1024,768]{1,0:T(8,128)(2,1)S(1)}, bf16[1024,768]{1,0:T(8,128)(2,1)}, u32[]{:S(2)}) copy-start(bf16[1024,768]{1,0:T(8,128)(2,1)} %get-tuple-element.30) | copy-start | bytes 4718596
  300.9 31.2 %copy-start.22 = (f32[768]{0:T(1024)S(1)}, f32[768]{0:T(1024)}, u32[]{:S(2)}) copy-start(f32[768]{0:T(1024)} %copy-done.21) | copy-start | bytes 9220
  302.2 29.9 %copy-start.5 = (bf16[1024,768]{1,0:T(8,128)(2,1)S(1)}, bf16[1024,768]{1,0:T(8,128)(2,1)}, u32[]{:S(2)}) copy-start(bf16[1024,768]{1,0:T(8,128)(2,1)} %copy-done.4) | copy-start | bytes 4718596
  302.2 29.9 %copy-start.9 = (bf16[1,2,512,768]{3,2,1,0:T(8,128)(2,1)S(1)}, bf16[1,2,512,768]{3,2,1,0:T(8,128)(2,1)}, u32[]{:S(2)}) copy-start(bf16[1,2,512,768]{3,2,1,0:T(8,128)(2,1)} %param.14) | copy-start | bytes 4718596
  302.2 29.9 %copy-start.16 = (bf16[1024,768]{1,0:T(8,128)(2,1)S(1)}, bf16[1024,768]{1,0:T(8,128)(2,1)}, u32[]{:S(2)}) copy-start(bf16[1024,768]{1,0:T(8,128)(2,1)} %get-tuple-element.77) | copy-start | bytes 4718596
  302.2 29.9 %copy-start.25 = (f32[1,4,2,128]{3,1,2,0:T(4,128)S(1)}, f32[1,4,2,128]{3,1,2,0:T(4,128)}, u32[]{:S(2)}) copy-start(f32[1,4,2,128]{3,1,2,0:T(4,128)} %copy.36) | copy-start | bytes 12292
  332.0 6.1 %copy-start.18 = (bf16[1024,768]{1,0:T(8,128)(2,1)}, bf16[1024,768]{1,0:T(8,128)(2,1)S(1)}, u32[]{:S(2)}) copy-start(bf16[1024,768]{1,0:T(8,128)(2,1)S(1)} %add_convert_fusion.3) | copy-start | bytes 4718596
  332.1 6.0 %copy-start.29 = (f32[1,768]{1,0:T(1,128)S(1)}, f32[1,768]{1,0:T(1,128)}, u32[]{:S(2)}) copy-start(f32[1,768]{1,0:T(1,128)} %reshape.303) | copy-start | bytes 9220
  340.7 5.2 copy-start.26
  340.7 5.2 copy-start.27
  340.7 5.2 copy-start.28
  533.8 7.0 %copy-start.14 = (bf16[768,3072]{1,0:T(8,128)(2,1)S(1)}, bf16[768,3072]{1,0:T(8,128)(2,1)}, u32[]{:S(2)}) copy-start(bf16[768,3072]{1,0:T(8,128)(2,1)} %get-tuple-element.36) | copy-start | bytes 14155780
  540.7 5.1 copy-start.15
  545.8 3.5 copy-start.19
